TPU v7x, 32 devices: a whole 2x2x4 slice. The times are simulated.
32 devices in a mesh: dp: 16 (over z, y, core), mp: 2 (over x).
Axes of the slice: x: 2, y: 2, z: 4, core: 2. Of those that a mesh axis runs over, the one named last changes fastest.
Arguments:
- tokens: bfloat16 [16384, 768], P(('dp', 'mp')), may hold values from -6 to 6
- norm1_gain: bfloat16 [768], replicated, may hold values from 0.25 to 1.75
- qkv_weight: bfloat16 [768, 3, 768], P('dp', None, 'mp'), may hold values from -0.21875 to 0.21875
- attn_out_weight: bfloat16 [768, 768], P('mp', 'dp'), may hold values from -1.75 to 1.75
- bias_table: bfloat16 [32, 12], replicated, may hold values from -4 to 4
- buckets: int32 [2047], replicated, may hold values from 0 to 31
- norm2_gain: bfloat16 [768], replicated, may hold values from 0.25 to 1.75
- router_weight: bfloat16 [768, 16], replicated, may hold values from -0.15917969 to 0.15917969
- routes: int32 [16384, 2], P('dp'), may hold values from 0 to 15, all different within a row; in each aligned block of 1024 rows (0 to 1023, 1024 to 2047, ...) at most 256 rows name the same one
- expert_in_weight: bfloat16 [16, 768, 3072], P('dp', None, 'mp'), may hold values from -0.21875 to 0.21875
- expert_out_weight: bfloat16 [16, 3072, 768], P('dp', 'mp'), may hold values from -0.109375 to 0.109375
- cotangent: bfloat16 [16384, 768], P(('dp', 'mp')), may hold values from -6 to 6
Outputs:
- mixed: bfloat16 [16384, 768], P(('dp', 'mp'))
- grad_tokens: float32 [16384, 768], P(('dp', 'mp'))
- grad_norm1_gain: float32 [768], replicated
- grad_qkv_weight: float32 [768, 3, 768], P('dp', None, 'mp')
- grad_attn_out_weight: float32 [768, 768], P('mp', 'dp')
- grad_bias_table: float32 [32, 12], replicated
- grad_norm2_gain: float32 [768], replicated
- grad_router_weight: float32 [768, 16], replicated
- grad_expert_in_weight: float32 [16, 768, 3072], P('dp', None, 'mp')
- grad_expert_out_weight: float32 [16, 3072, 768], P('dp', 'mp')
Inputs may be any that keep to these rules, and one draw needn't show every extreme that they name: `routes`: the two experts of a token differ. In each aligned block of 1024 rows no expert is named by more than 256 rows, and in some blocks one expert is named by exactly 256.
All inputs are finite; a program needn't handle non-finite values.
Results may differ from a plain program's by a relative error of at most 0.015.
Values may be sent and summed in bfloat16 or wider, within the bound.
No kernel may reach another device: no remote copies, remote signals or barrier semaphores. Data moves between devices by JAX's collectives and lax.ppermute only.
A program may use at most 256 MiB of HBM per device.

v0:
```python
from functools import partial

import jax
import jax.numpy as jnp
from jax import lax
from jax.sharding import PartitionSpec as P

HDIM = 64
NBUCKET = 32
BLOCK = 256


EPSILON = 1e-06
MASKED = -1e30


def rms_scale(values):
    return lax.rsqrt(jnp.mean(values * values, axis=-1, keepdims=True) + EPSILON)


def norm_back(values, scale, gain, upstream):
    normed = values * scale
    weighted = upstream * gain
    return scale * (weighted - normed * jnp.mean(weighted * normed, axis=-1, keepdims=True))


def contract_rows(left, right):
    return lax.dot_general(
        left, right, (((0,), (0,)), ((), ())), preferred_element_type=jnp.float32
    )


def times_transpose(left, right):
    return lax.dot_general(
        left, right, (((1,), (1,)), ((), ())), preferred_element_type=jnp.float32
    )


def tile_bias(offsets, tile_rows, key_rows, seq_len):
    span_cols = tile_rows + key_rows
    window = lax.slice_in_dim(
        offsets, seq_len - tile_rows, seq_len - tile_rows + span_cols + 1, axis=1
    )[:, ::-1]
    head_count = offsets.shape[0]
    spread = jnp.broadcast_to(window[:, None, :], (head_count, tile_rows, span_cols + 1))
    flattened = spread.reshape(head_count, tile_rows * (span_cols + 1))[:, : tile_rows * span_cols]
    return flattened.reshape(head_count, tile_rows, span_cols)[:, :, tile_rows:]


def tile_allowed(first_row, tile_rows, key_rows):
    row_block = (first_row + jnp.arange(tile_rows)) // BLOCK
    col_block = jnp.arange(key_rows) // BLOCK
    return col_block[None, :] <= row_block[:, None]


def attend_forward(queries, keys_all, values, offsets):
    seq_len = queries.shape[1]
    tile_rows = min(512, seq_len)
    outputs = []
    log_sums = []
    for first_row in range(0, seq_len, tile_rows):
        key_rows = first_row + tile_rows
        scores = (
            jnp.einsum(
                "hqd,hkd->hqk",
                queries[:, first_row:key_rows],
                keys_all[:, :key_rows],
                preferred_element_type=jnp.float32,
            )
            * 0.125
        )
        scores = scores + tile_bias(offsets, tile_rows, key_rows, seq_len)
        scores = jnp.where(tile_allowed(first_row, tile_rows, key_rows)[None], scores, MASKED)
        row_max = jnp.max(scores, axis=-1, keepdims=True)
        exponent = jnp.exp(scores - row_max)
        row_sum = jnp.sum(exponent, axis=-1, keepdims=True)
        weights_low = (exponent / row_sum).astype(jnp.bfloat16)
        outputs.append(
            jnp.einsum(
                "hqk,hkd->hqd",
                weights_low,
                values[:, :key_rows],
                preferred_element_type=jnp.float32,
            )
        )
        log_sums.append((row_max + jnp.log(row_sum))[..., 0])
    return (jnp.concatenate(outputs, axis=1), jnp.concatenate(log_sums, axis=1))


def attend_backward(queries, keys_all, values, grad_out, log_sums, offsets):
    seq_len = queries.shape[1]
    tile_rows = min(512, seq_len)
    grad_queries = []
    grad_keys = jnp.zeros(keys_all.shape, jnp.float32)
    grad_values = jnp.zeros(values.shape, jnp.float32)
    grad_offsets = jnp.zeros(offsets.shape, jnp.float32)
    for first_row in range(0, seq_len, tile_rows):
        key_rows = first_row + tile_rows
        bias_tile, bias_back = jax.vjp(
            partial(tile_bias, tile_rows=tile_rows, key_rows=key_rows, seq_len=seq_len), offsets
        )
        scores = (
            jnp.einsum(
                "hqd,hkd->hqk",
                queries[:, first_row:key_rows],
                keys_all[:, :key_rows],
                preferred_element_type=jnp.float32,
            )
            * 0.125
        )
        scores = jnp.where(
            tile_allowed(first_row, tile_rows, key_rows)[None], scores + bias_tile, MASKED
        )
        weights = jnp.exp(scores - log_sums[:, first_row:key_rows, None])
        weights_low = weights.astype(jnp.bfloat16)
        grad_tile = grad_out[:, first_row:key_rows]
        grad_values = grad_values.at[:, :key_rows].add(
            jnp.einsum("hqk,hqd->hkd", weights_low, grad_tile, preferred_element_type=jnp.float32)
        )
        grad_weights = jnp.einsum(
            "hqd,hkd->hqk", grad_tile, values[:, :key_rows], preferred_element_type=jnp.float32
        )
        grad_scores = (
            weights * (grad_weights - jnp.sum(grad_weights * weights, axis=-1, keepdims=True))
        ).astype(jnp.bfloat16)
        grad_queries.append(
            jnp.einsum(
                "hqk,hkd->hqd",
                grad_scores,
                keys_all[:, :key_rows],
                preferred_element_type=jnp.float32,
            )
            * 0.125
        )
        grad_keys = grad_keys.at[:, :key_rows].add(
            jnp.einsum(
                "hqk,hqd->hkd",
                grad_scores,
                queries[:, first_row:key_rows],
                preferred_element_type=jnp.float32,
            )
            * 0.125
        )
        grad_offsets = grad_offsets + bias_back(grad_scores.astype(jnp.float32))[0]
    return (jnp.concatenate(grad_queries, axis=1), grad_keys, grad_values, grad_offsets)


def head_major(block, head_count):
    return block.reshape(block.shape[0], head_count, -1).transpose(1, 0, 2)


def token_major(block):
    return block.transpose(1, 0, 2).reshape(block.shape[1], -1)


def expert_major(block, local_count):
    sources = block.shape[0] // local_count
    cap_rows = block.shape[1]
    return (
        block.reshape(sources, local_count, cap_rows, -1)
        .transpose(1, 0, 2, 3)
        .reshape(local_count, sources * cap_rows, -1)
    )


def source_major(block, sources):
    local_count = block.shape[0]
    cap_rows = block.shape[1] // sources
    return (
        block.reshape(local_count, sources, cap_rows, -1)
        .transpose(1, 0, 2, 3)
        .reshape(sources * local_count, cap_rows, -1)
    )


def per_device(
    tokens,
    norm1_gain,
    qkv_weight,
    attn_out_weight,
    bias_table,
    buckets,
    norm2_gain,
    router_weight,
    routes,
    expert_in_weight,
    expert_out_weight,
    cotangent,
):
    model_rank = lax.axis_index("mp")
    local_rows, width = tokens.shape
    group_rows = routes.shape[0]
    expert_total = router_weight.shape[1]
    local_experts = expert_in_weight.shape[0]
    sources = expert_total // local_experts
    capacity = 4 * group_rows // expert_total
    head_local = qkv_weight.shape[2] // HDIM
    own_start = model_rank * local_rows
    gain_one = norm1_gain.astype(jnp.float32)
    gain_two = norm2_gain.astype(jnp.float32)
    token_f = tokens.astype(jnp.float32)
    scale_one = rms_scale(token_f)
    normed_one = (token_f * scale_one * gain_one).astype(jnp.bfloat16)
    normed_all = lax.all_gather(normed_one, "mp", axis=0, tiled=True)
    qkv_full, attn_out_full = (
        lax.all_gather(qkv_weight, "dp", axis=0, tiled=True),
        lax.all_gather(attn_out_weight, "dp", axis=1, tiled=True),
    )
    qkv_vals = jnp.einsum(
        "td,dch->tch", normed_all, qkv_full, preferred_element_type=jnp.float32
    ).astype(jnp.bfloat16)
    own_table = lax.dynamic_slice_in_dim(
        bias_table.astype(jnp.float32), model_rank * head_local, head_local, 1
    )
    bucket_hot = (buckets[:, None] == jnp.arange(NBUCKET)[None, :]).astype(jnp.float32)
    offsets = jnp.pad(
        jnp.dot(bucket_hot, own_table, precision=lax.Precision.HIGHEST).T, ((0, 0), (1, 1))
    )
    attended_seq, log_seq = attend_forward(
        head_major(qkv_vals[:, 0], head_local),
        head_major(qkv_vals[:, 1], head_local),
        head_major(qkv_vals[:, 2], head_local),
        offsets,
    )
    attn_rows = token_major(attended_seq)
    attended = attn_rows.astype(jnp.bfloat16)
    branch_part = jnp.dot(attended, attn_out_full, preferred_element_type=jnp.float32)
    with_tokens = lax.dynamic_update_slice_in_dim(
        branch_part,
        lax.dynamic_slice_in_dim(branch_part, own_start, local_rows, 0) + token_f,
        own_start,
        0,
    )
    mid_all = lax.psum(with_tokens, "mp")
    scale_two = rms_scale(mid_all)
    moe_in = (mid_all * scale_two * gain_two).astype(jnp.bfloat16)
    logits = jnp.dot(moe_in, router_weight, preferred_element_type=jnp.float32)
    router_probs = jax.nn.softmax(logits, axis=-1)
    expert_ids = jnp.arange(expert_total)
    route_hot = (routes[:, :, None] == expert_ids[None, None, :]).astype(jnp.float32)
    selected = jnp.sum(route_hot * router_probs[:, None, :], axis=-1)
    pair_sum = jnp.sum(selected, axis=1, keepdims=True)
    gate_vals = selected / pair_sum
    flat_routes = routes.reshape(-1)
    flat_hot = (flat_routes[:, None] == expert_ids[None, :]).astype(jnp.int32)
    slot_ranks = jnp.sum(jnp.cumsum(flat_hot, axis=0) * flat_hot, axis=1) - 1
    slot_index = flat_routes * capacity + slot_ranks
    assign_ids = jnp.arange(2 * group_rows, dtype=jnp.int32)
    source_assign = (
        jnp.full((expert_total * capacity,), 2 * group_rows, jnp.int32)
        .at[slot_index]
        .set(assign_ids)
    )
    slot_tokens = source_assign // 2
    moe_pad = jnp.concatenate([moe_in, jnp.zeros((1, width), jnp.bfloat16)], axis=0)
    send_rows = moe_pad[slot_tokens].reshape(expert_total, capacity, width)

    def to_experts(buffer):
        whole = lax.all_to_all(buffer, "dp", split_axis=0, concat_axis=0, tiled=True)
        return expert_major(whole, local_experts)

    def to_tokens(partial_rows):
        ordered = source_major(partial_rows, sources)
        back = lax.all_to_all(ordered, "dp", split_axis=0, concat_axis=0, tiled=True)
        rows_back = back.reshape(expert_total * capacity, width)[slot_index].astype(jnp.float32)
        return rows_back.reshape(group_rows, 2, width)

    expert_rows = to_experts(send_rows)
    row_total = expert_rows.shape[1]
    block_rows = min(2048, row_total)
    expert_local = 0
    blocks_out = []
    for start_row in range(0, row_total, block_rows):
        inputs_blk = expert_rows[expert_local, start_row : start_row + block_rows]
        hidden_before_activation = jnp.dot(
            inputs_blk, expert_in_weight[expert_local], preferred_element_type=jnp.float32
        )
        hidden_activation = jax.nn.gelu(hidden_before_activation).astype(jnp.bfloat16)
        blocks_out.append(
            jnp.dot(
                hidden_activation,
                expert_out_weight[expert_local],
                preferred_element_type=jnp.float32,
            ).astype(jnp.bfloat16)
        )
    expert_blocks = [jnp.concatenate(blocks_out, axis=0)]
    expert_result = jnp.stack(expert_blocks, axis=0)
    picked = to_tokens(expert_result)
    moe_part = gate_vals[:, 0:1] * picked[:, 0] + gate_vals[:, 1:2] * picked[:, 1]
    moe_rows = lax.psum_scatter(
        moe_part.astype(jnp.bfloat16), "mp", scatter_dimension=0, tiled=True
    ).astype(jnp.float32)
    mid_own = lax.dynamic_slice_in_dim(mid_all, own_start, local_rows, 0)
    mixed = (mid_own + moe_rows).astype(jnp.bfloat16)
    grad_all = lax.all_gather(cotangent, "mp", axis=0, tiled=True).astype(jnp.float32)
    grad_pad = jnp.concatenate([grad_all, jnp.zeros((1, width), jnp.float32)], axis=0)
    gate_pad = jnp.concatenate([gate_vals.reshape(-1), jnp.zeros((1,), jnp.float32)], axis=0)
    send_grad = (
        (grad_pad[slot_tokens] * gate_pad[source_assign][:, None])
        .astype(jnp.bfloat16)
        .reshape(expert_total, capacity, width)
    )
    gate_grad_part = jnp.sum(grad_all[:, None, :] * picked, axis=-1)
    grad_rows = to_experts(send_grad)
    rows_again = to_experts(send_rows)
    expert_local = 0
    input_weight = expert_in_weight[expert_local]
    output_weight = expert_out_weight[expert_local]
    acc_in = jnp.zeros(input_weight.shape, jnp.float32)
    acc_out = jnp.zeros(output_weight.shape, jnp.float32)
    din_blocks = []
    for start_row in range(0, row_total, block_rows):
        inputs_blk = rows_again[expert_local, start_row : start_row + block_rows]
        dout_blk = grad_rows[expert_local, start_row : start_row + block_rows]
        hidden_before_activation = jnp.dot(
            inputs_blk, input_weight, preferred_element_type=jnp.float32
        )
        act_value, gelu_back = jax.vjp(jax.nn.gelu, hidden_before_activation)
        hidden_activation = act_value.astype(jnp.bfloat16)
        grad_act = times_transpose(dout_blk, output_weight)
        grad_pre = gelu_back(grad_act)[0].astype(jnp.bfloat16)
        acc_out = acc_out + contract_rows(hidden_activation, dout_blk)
        acc_in = acc_in + contract_rows(inputs_blk, grad_pre)
        din_blocks.append(times_transpose(grad_pre, input_weight).astype(jnp.bfloat16))
    in_grads = [acc_in]
    out_grads = [acc_out]
    din_experts = [jnp.concatenate(din_blocks, axis=0)]
    din_local = jnp.stack(din_experts, axis=0)
    din_picked = to_tokens(din_local)
    dmoe_part = din_picked[:, 0] + din_picked[:, 1]
    dmoe_sum, gate_grad = lax.psum((dmoe_part, gate_grad_part), "mp")
    dselected = (gate_grad - jnp.sum(gate_grad * gate_vals, axis=1, keepdims=True)) / pair_sum
    dprobs_router = jnp.sum(route_hot * dselected[:, :, None], axis=1)
    dlogits = (
        router_probs
        * (dprobs_router - jnp.sum(dprobs_router * router_probs, axis=-1, keepdims=True))
    ).astype(jnp.bfloat16)
    dmoe_in = dmoe_sum + times_transpose(dlogits, router_weight)
    own_moe = lax.dynamic_slice_in_dim(moe_in, own_start, local_rows, 0)
    own_dlogits = lax.dynamic_slice_in_dim(dlogits, own_start, local_rows, 0)
    router_grad = contract_rows(own_moe, own_dlogits)
    own_dmoe = lax.dynamic_slice_in_dim(dmoe_in, own_start, local_rows, 0)
    own_scale_two = lax.dynamic_slice_in_dim(scale_two, own_start, local_rows, 0)
    gain2_grad = jnp.sum(own_dmoe * mid_own * own_scale_two, axis=0)
    dmid = grad_all + norm_back(mid_all, scale_two, gain_two, dmoe_in)
    dbranch = dmid.astype(jnp.bfloat16)
    attn_out_grad = contract_rows(attended, dbranch)
    dattended = times_transpose(dbranch, attn_out_full).astype(jnp.bfloat16)
    grad_seq = head_major(dattended, head_local)
    grad_query, grad_key, grad_value, grad_off = attend_backward(
        head_major(qkv_vals[:, 0], head_local),
        head_major(qkv_vals[:, 1], head_local),
        head_major(qkv_vals[:, 2], head_local),
        grad_seq,
        log_seq,
        offsets,
    )
    dqkv_parts = jnp.stack(
        [token_major(grad_query), token_major(grad_key), token_major(grad_value)], axis=1
    )
    dqkv = dqkv_parts.astype(jnp.bfloat16)
    qkv_grad = jnp.einsum("td,tch->dch", normed_all, dqkv, preferred_element_type=jnp.float32)
    dnormed_part = jnp.einsum("tch,dch->td", dqkv, qkv_full, preferred_element_type=jnp.float32)
    dnormed = lax.psum_scatter(
        dnormed_part.astype(jnp.bfloat16), "mp", scatter_dimension=0, tiled=True
    ).astype(jnp.float32)
    gain1_grad = jnp.sum(dnormed * token_f * scale_one, axis=0)
    dmid_own = lax.dynamic_slice_in_dim(dmid, own_start, local_rows, 0)
    grad_tokens = dmid_own + norm_back(token_f, scale_one, gain_one, dnormed)
    qkv_grad_own, attn_out_grad_own = (
        lax.psum_scatter(qkv_grad, "dp", scatter_dimension=0, tiled=True),
        lax.psum_scatter(attn_out_grad, "dp", scatter_dimension=1, tiled=True),
    )
    own_table_grad = lax.dot_general(
        bucket_hot,
        grad_off[:, 1:-1],
        (((0,), (1,)), ((), ())),
        precision=lax.Precision.HIGHEST,
        preferred_element_type=jnp.float32,
    )
    table_grad = lax.dynamic_update_slice_in_dim(
        jnp.zeros((NBUCKET, bias_table.shape[1]), jnp.float32),
        own_table_grad,
        model_rank * head_local,
        1,
    )
    gain1_total, gain2_total, table_total, router_total = lax.psum(
        (gain1_grad, gain2_grad, table_grad, router_grad), ("dp", "mp")
    )
    return (
        mixed,
        grad_tokens,
        gain1_total,
        qkv_grad_own,
        attn_out_grad_own,
        table_total,
        gain2_total,
        router_total,
        jnp.stack(in_grads, axis=0),
        jnp.stack(out_grads, axis=0),
    )


def solution(mesh):
    placed = (
        P(("dp", "mp"), None),
        P(),
        P("dp", None, "mp"),
        P("mp", "dp"),
        P(),
        P(),
        P(),
        P(),
        P("dp", None),
        P("dp", None, "mp"),
        P("dp", "mp", None),
        P(("dp", "mp"), None),
    )
    return jax.shard_map(
        per_device,
        mesh=mesh,
        in_specs=placed,
        out_specs=(
            P(("dp", "mp"), None),
            P(("dp", "mp"), None),
            P(),
            P("dp", None, "mp"),
            P("mp", "dp"),
            P(),
            P(),
            P(),
            P("dp", None, "mp"),
            P("dp", "mp", None),
        ),
        check_vma=False,
    )
```

profile of v0, /device:TPU:0, one launch (start us, length us, event | category | flops | bytes accessed | tf_op | source)
XLA Modules:
  0.0 2333.7 jit_solution(16700872303182246690)
XLA Ops:
  24.6 30.3 %reshape.549 = f32[4721664]{0:T(1024)} reshape(f32[6,512,1537]{2,1,0:T(8,128)} %broadcast_in_dim.48) | data formatting | bytes 37773312
  54.9 466.9 %while.8 = (u32[]{:T(128)}, f32[4721664]{0:T(1024)}, f32[1,6,786944]{2,1,0:T(8,128)}, u32[]{}, u32[]{}, /*index=5*/u32[]{}, u32[]{}, u32[]{}) while((u32[]{:T(128)}, f32[4721664]{0:T(1024)}, f32[1,6,786944]{2,1,0:T(8,128)}, u32[]{}, u32[]{}, /*index=5*/u32[]{}, u32[]{}, u32[]{}) %tuple.68), condition=%wide.cond, body=%wide.body.sunk | while | flops 9 | bytes 18886832
  73.1 59.5 %dynamic-update-slice.14 = f32[1,6,786944]{2,1,0:T(8,128)} dynamic-update-slice(f32[1,6,786944]{2,1,0:T(8,128)} %get-tuple-element.181, f32[1,1,786944]{2,1,0:T(1,128)} %reshape.560, u32[]{:T(128)S(6)} %multiply.49, u32[]{:T(128)S(6)} %multiply.51, u32[]{} %constant.444..sunk) | dynamic-update-slice | bytes 6295556
  151.0 59.5 %dynamic-update-slice.14 = f32[1,6,786944]{2,1,0:T(8,128)} dynamic-update-slice(f32[1,6,786944]{2,1,0:T(8,128)} %get-tuple-element.181, f32[1,1,786944]{2,1,0:T(1,128)} %reshape.560, u32[]{:T(128)S(6)} %multiply.49, u32[]{:T(128)S(6)} %multiply.51, u32[]{} %constant.444..sunk) | dynamic-update-slice | bytes 6295556
  228.8 59.5 %dynamic-update-slice.14 = f32[1,6,786944]{2,1,0:T(8,128)} dynamic-update-slice(f32[1,6,786944]{2,1,0:T(8,128)} %get-tuple-element.181, f32[1,1,786944]{2,1,0:T(1,128)} %reshape.560, u32[]{:T(128)S(6)} %multiply.49, u32[]{:T(128)S(6)} %multiply.51, u32[]{} %constant.444..sunk) | dynamic-update-slice | bytes 6295556
  306.6 59.5 %dynamic-update-slice.14 = f32[1,6,786944]{2,1,0:T(8,128)} dynamic-update-slice(f32[1,6,786944]{2,1,0:T(8,128)} %get-tuple-element.181, f32[1,1,786944]{2,1,0:T(1,128)} %reshape.560, u32[]{:T(128)S(6)} %multiply.49, u32[]{:T(128)S(6)} %multiply.51, u32[]{} %constant.444..sunk) | dynamic-update-slice | bytes 6295556
  384.4 59.5 %dynamic-update-slice.14 = f32[1,6,786944]{2,1,0:T(8,128)} dynamic-update-slice(f32[1,6,786944]{2,1,0:T(8,128)} %get-tuple-element.181, f32[1,1,786944]{2,1,0:T(1,128)} %reshape.560, u32[]{:T(128)S(6)} %multiply.49, u32[]{:T(128)S(6)} %multiply.51, u32[]{} %constant.444..sunk) | dynamic-update-slice | bytes 6295556
  462.2 59.5 %dynamic-update-slice.14 = f32[1,6,786944]{2,1,0:T(8,128)} dynamic-update-slice(f32[1,6,786944]{2,1,0:T(8,128)} %get-tuple-element.181, f32[1,1,786944]{2,1,0:T(1,128)} %reshape.560, u32[]{:T(128)S(6)} %multiply.49, u32[]{:T(128)S(6)} %multiply.51, u32[]{} %constant.444..sunk) | dynamic-update-slice | bytes 6295556
  707.5 68.4 %all-reduce.15.cloned.1.call-done = f32[1024,768]{1,0:T(8,128)} async-done(((f32[1024,768]{1,0:T(8,128)}), f32[1024,768]{1,0:T(8,128)}) %all-reduce.15.cloned.1.call-update) | async-done | bytes 3145744 | tf_op jit(solution)/shard_map/psum | solution.py:234
  803.4 143.2 %all_to_all.21 = bf16[16,256,768]{2,1,0:T(8,128)(2,1)S(1)} all-to-all(bf16[16,256,768]{2,1,0:T(8,128)(2,1)} %bitcast.171), channel_id=1, replica_groups=mesh['dp'=16,'mp'=2] {'dp'}, dimensions={0} | all-to-all | bytes 12582912 | tf_op jit(solution)/shard_map/all_to_all | solution.py:259
  987.3 29.1 %all-gather.8.cloned.1.call-done = bf16[1024,768]{1,0:T(8,128)(2,1)} async-done(((bf16[512,768]{1,0:T(8,128)(2,1)}), bf16[1024,768]{1,0:T(8,128)(2,1)}) %all-gather.8.cloned.1.call-update) | async-done | bytes 1572880 | tf_op jit(solution)/shard_map/all_gather | solution.py:295
  1047.7 53.2 %all-to-all-done.1 = bf16[16,256,768]{2,1,0:T(8,128)(2,1)} async-done(((bf16[16,256,768]{2,1,0:T(8,128)(2,1)}), bf16[16,256,768]{2,1,0:T(8,128)(2,1)}, u32[]{:S(2)}, u32[]{:S(2)}) %all-to-all-start.1) | async-done | bytes 6291488 | tf_op jit(solution)/shard_map/all_to_all | solution.py:264
  1176.8 165.4 %all_to_all.22 = bf16[16,256,768]{2,1,0:T(8,128)(2,1)S(1)} all-to-all(bf16[16,256,768]{2,1,0:T(8,128)(2,1)} %multiply_convert_fusion.1), channel_id=1, replica_groups=mesh['dp'=16,'mp'=2] {'dp'}, dimensions={0} | all-to-all | bytes 12582912 | tf_op jit(solution)/shard_map/all_to_all | solution.py:259
  1392.4 143.0 %all_to_all.23 = bf16[16,256,768]{2,1,0:T(8,128)(2,1)} all-to-all(bf16[16,256,768]{2,1,0:T(8,128)(2,1)S(1)} %bitcast.168), channel_id=1, replica_groups=mesh['dp'=16,'mp'=2] {'dp'}, dimensions={0} | all-to-all | bytes 12582912 | tf_op jit(solution)/shard_map/all_to_all | solution.py:264
  1625.3 35.3 %all-reduce.17.cloned.1.call-done = f32[1024,768]{1,0:T(8,128)} async-done(((f32[1024,768]{1,0:T(8,128)}), f32[1024,768]{1,0:T(8,128)}) %all-reduce.17.cloned.1.call-update) | async-done | bytes 3145744 | tf_op jit(solution)/shard_map/psum | solution.py:331
  1803.9 391.3 %while.9 = (u32[]{:T(128)}, f32[1,6,786944]{2,1,0:T(8,128)}, f32[4721664]{0:T(1024)}, u32[]{}, f32[]{:T(128)}, /*index=5*/u32[]{}, u32[]{}, u32[]{}) while((u32[]{:T(128)}, f32[1,6,786944]{2,1,0:T(8,128)}, f32[4721664]{0:T(1024)}, u32[]{}, f32[]{:T(128)}, /*index=5*/u32[]{}, u32[]{}, u32[]{}) %tuple.71), condition=%wide.cond.1, body=%wide.body.1.sunk | while | flops 9 | bytes 12591297
  1804.6 36.9 %dynamic-slice_reduce_fusion.2 = f32[786944]{0:T(1024)} fusion(f32[]{:T(128)} %broadcast.567, f32[1,6,786944]{2,1,0:T(8,128)} %get-tuple-element.212, u32[]{:T(128)S(6)} %multiply.53, u32[]{:T(128)S(6)} %multiply.54), kind=kLoop, calls=%fused_computation.241.clone.1 | loop fusion | bytes 6295564
  1869.9 36.8 %dynamic-slice_reduce_fusion.2 = f32[786944]{0:T(1024)} fusion(f32[]{:T(128)} %broadcast.567, f32[1,6,786944]{2,1,0:T(8,128)} %get-tuple-element.212, u32[]{:T(128)S(6)} %multiply.53, u32[]{:T(128)S(6)} %multiply.54), kind=kLoop, calls=%fused_computation.241.clone.1 | loop fusion | bytes 6295564
  1935.1 36.8 %dynamic-slice_reduce_fusion.2 = f32[786944]{0:T(1024)} fusion(f32[]{:T(128)} %broadcast.567, f32[1,6,786944]{2,1,0:T(8,128)} %get-tuple-element.212, u32[]{:T(128)S(6)} %multiply.53, u32[]{:T(128)S(6)} %multiply.54), kind=kLoop, calls=%fused_computation.241.clone.1 | loop fusion | bytes 6295564
  2000.3 36.8 %dynamic-slice_reduce_fusion.2 = f32[786944]{0:T(1024)} fusion(f32[]{:T(128)} %broadcast.567, f32[1,6,786944]{2,1,0:T(8,128)} %get-tuple-element.212, u32[]{:T(128)S(6)} %multiply.53, u32[]{:T(128)S(6)} %multiply.54), kind=kLoop, calls=%fused_computation.241.clone.1 | loop fusion | bytes 6295564
  2065.5 36.8 %dynamic-slice_reduce_fusion.2 = f32[786944]{0:T(1024)} fusion(f32[]{:T(128)} %broadcast.567, f32[1,6,786944]{2,1,0:T(8,128)} %get-tuple-element.212, u32[]{:T(128)S(6)} %multiply.53, u32[]{:T(128)S(6)} %multiply.54), kind=kLoop, calls=%fused_computation.241.clone.1 | loop fusion | bytes 6295564
  2130.7 36.8 %dynamic-slice_reduce_fusion.2 = f32[786944]{0:T(1024)} fusion(f32[]{:T(128)} %broadcast.567, f32[1,6,786944]{2,1,0:T(8,128)} %get-tuple-element.212, u32[]{:T(128)S(6)} %multiply.53, u32[]{:T(128)S(6)} %multiply.54), kind=kLoop, calls=%fused_computation.241.clone.1 | loop fusion | bytes 6295564
  2195.2 31.1 %reshape.489 = f32[6,512,1537]{2,1,0:T(8,128)} reshape(f32[4721664]{0:T(1024)} %get-tuple-element.83) | data formatting | bytes 37773312 | tf_op jit(solution)/shard_map/transpose(jvp())/reshape | solution.py:46
  2282.9 40.6 %all-reduce.11 = (f32[768]{0:T(1024)}, f32[32,12]{0,1:T(8,128)}, f32[768]{0:T(1024)}, f32[768,16]{0,1:T(8,128)}) all-reduce(f32[768]{0:T(1024)S(1)} %get-tuple-element.84, f32[32,12]{0,1:T(8,128)S(1)} %dynamic_update_slice.7, f32[768]{0:T(1024)S(1)} %get-tuple-element.110, ...), channel_id=1, replica_groups=mesh['dp'=16,'mp'=2] {'dp','mp'}, use_global_device_ids=true, to_apply=%region_28.29 | all-reduce | flops 14208 | bytes 113664 | tf_op jit(solution)/shard_map/psum | solution.py:387
  (330 shorter events, 1000.6 us)
Async XLA Ops:
  7.2 952.8 %copy-start = (bf16[1,1536,768]{2,1,0:T(8,128)(2,1)S(1)}, bf16[1,1536,768]{2,1,0:T(8,128)(2,1)}, u32[]{:S(2)}) copy-start(bf16[1,1536,768]{2,1,0:T(8,128)(2,1)} %param.34) | copy-start | bytes 7077892
  7.2 654.1 %all-gather.4.cloned.1.call-start = ((), (), s32[]{:S(2)}) async-start(), calls=%async_computation.8 | async-start | bytes 2359296 | tf_op jit(solution)/shard_map/all_gather | solution.py:204
  12.3 649.0 %all-gather.6.cloned.1.call-start = ((), (), s32[]{:S(2)}) async-start(), calls=%async_computation.9 | async-start | bytes 1880064 | tf_op jit(solution)/shard_map/all_gather | solution.py:206
  13.1 762.8 %all-reduce.15.cloned.1.call-start = ((), (), s32[]{:S(2)}) async-start(), calls=%async_computation.10 | async-start | bytes 6291456 | tf_op jit(solution)/shard_map/psum | solution.py:234
  661.3 25.0 %copy-start.21 = (bf16[384,768]{0,1:T(8,128)(2,1)}, bf16[384,768]{0,1:T(8,128)(2,1)S(1)}, u32[]{:S(2)}) copy-start(bf16[384,768]{0,1:T(8,128)(2,1)S(1)} %all_gather.14) | copy-start | bytes 1769476
  665.8 16.1 copy-start.13
  665.8 16.1 copy-start.15
  665.8 18.7 copy-start.23
  693.5 89.2 %copy-start.39 = (f32[768]{0:T(1024)}, f32[768]{0:T(1024)S(1)}, u32[]{:S(2)}) copy-start(f32[768]{0:T(1024)S(1)} %convert_element_type.139) | copy-start | bytes 9220
  778.1 25.3 %copy-start.35 = (f32[1024]{0:T(1024)}, f32[1024]{0:T(1024)S(1)}, u32[]{:S(2)}) copy-start(f32[1024]{0:T(1024)S(1)} %add_rsqrt_fusion) | copy-start | bytes 12292
  803.4 143.2 %copy-start.50 = (bf16[1,768,1536]{2,1,0:T(8,128)(2,1)S(1)}, bf16[1,768,1536]{2,1,0:T(8,128)(2,1)}, u32[]{:S(2)}) copy-start(bf16[1,768,1536]{2,1,0:T(8,128)(2,1)} %param.33) | copy-start | bytes 7077892
  981.1 119.7 %all-to-all-start.1 = ((bf16[16,256,768]{2,1,0:T(8,128)(2,1)}), bf16[16,256,768]{2,1,0:T(8,128)(2,1)}, u32[]{:S(2)}, u32[]{:S(2)}) async-start(bf16[16,256,768]{2,1,0:T(8,128)(2,1)} %bitcast.167), calls=%async_computation.1 | async-start | bytes 12582912 | tf_op jit(solution)/shard_map/all_to_all | solution.py:264
  986.7 29.7 %all-gather.8.cloned.1.call-start = ((), (), s32[]{:S(2)}) async-start(), calls=%async_computation.12 | async-start | bytes 2359296 | tf_op jit(solution)/shard_map/all_gather | solution.py:295
  987.3 673.3 %all-reduce.17.cloned.1.call-start = ((), (), s32[]{:S(2)}) async-start(), calls=%async_computation.13 | async-start | bytes 6291456 | tf_op jit(solution)/shard_map/psum | solution.py:331
  1019.7 25.9 %copy-start.33 = (bf16[768,16]{0,1:T(8,128)(2,1)S(1)}, bf16[768,16]{0,1:T(8,128)(2,1)}, u32[]{:S(2)}) copy-start(bf16[768,16]{0,1:T(8,128)(2,1)} %param.31) | copy-start | bytes 73732
  1342.2 17.6 copy-start.20
  1574.7 703.2 %reduce-scatter.5.cloned.1.call-start = ((), (), s32[]{:S(2)}) async-start(), calls=%async_computation.11 | async-start | bytes 2359296 | tf_op jit(solution)/shard_map/reduce_scatter | solution.py:290
  1594.6 686.5 %reduce-scatter.7.cloned.1.call-start = ((), (), s32[]{:S(2)}) async-start(), calls=%async_computation.14 | async-start | bytes 2359296 | tf_op jit(solution)/shard_map/reduce_scatter | solution.py:364
  1615.0 45.5 %copy-start.34 = (bf16[768,16]{0,1:T(8,128)(2,1)S(1)}, bf16[768,16]{0,1:T(8,128)(2,1)}, u32[]{:S(2)}) copy-start(bf16[768,16]{0,1:T(8,128)(2,1)} %param.31) | copy-start | bytes 73732
  1615.0 45.5 %copy-start.40 = (f32[768]{0:T(1024)S(1)}, f32[768]{0:T(1024)}, u32[]{:S(2)}) copy-start(f32[768]{0:T(1024)} %copy-done.39) | copy-start | bytes 9220
  1625.3 40.9 %copy-start.12 = (bf16[1024,768]{1,0:T(8,128)(2,1)S(1)}, bf16[1024,768]{1,0:T(8,128)(2,1)}, u32[]{:S(2)}) copy-start(bf16[1024,768]{1,0:T(8,128)(2,1)} %all-gather.8.cloned.1.call-done) | copy-start | bytes 4718596
  1725.8 600.9 %reduce-scatter.11.cloned.1.call-start = ((), (), s32[]{:S(2)}) async-start(), calls=%async_computation.16 | async-start | bytes 1253376 | tf_op jit(solution)/shard_map/reduce_scatter | solution.py:372
  1761.0 565.8 %reduce-scatter.9.cloned.1.call-start = ((), (), s32[]{:S(2)}) async-start(), calls=%async_computation.15 | async-start | bytes 3760128 | tf_op jit(solution)/shard_map/reduce_scatter | solution.py:371
  2270.4 56.3 %copy-start.1 = (bf16[1,1536,768]{2,1,0:T(8,128)(2,1)S(1)}, bf16[1,1536,768]{2,1,0:T(8,128)(2,1)}, u32[]{:S(2)}) copy-start(bf16[1,1536,768]{2,1,0:T(8,128)(2,1)} %param.34) | copy-start | bytes 7077892
  (48 other events, 302.2 us)
Sparse Core Ops, SparseCore 0:
  12.5 29.8 all-gather.3
  44.7 40.4 all-gather.5
  692.8 83.0 all-reduce.14
  988.8 27.5 all-gather.7
  1574.8 85.6 all-reduce.16
  1663.2 26.0 reduce-scatter.4
  1725.9 26.0 reduce-scatter.6
  1761.1 58.0 reduce-scatter.10
  1823.6 67.0 reduce-scatter.8
where the time goes:
time: 2360 us; the launch traced here: 2330 us
  local copies, waits for them, and re-layouts  1280 us (54%)
  blocking collectives  522 us (22%)
  matrix products  196 us (8%)
  waiting for transfers between devices  187 us (8%)
  other arithmetic  129 us (5%)
    unnamed x180, local copies, waits for them, and re-layouts  1010 us
    all_to_all x2, blocking collectives, to_experts(): lax.all_to_all(buffer, 'dp', split_axis=0, concat_axis=0, tiled=True)  309 us
    all_to_all x1, blocking collectives, to_tokens(): lax.all_to_all(ordered, 'dp', split_axis=0, concat_axis=0, tiled=True)  143 us
    psum x1, waiting for transfers between devices, per_device(): mid_all = lax.psum(with_tokens, 'mp')  68.4 us
    reshape x3, local copies, waits for them, and re-layouts, tile_bias(): spread.reshape(head_count, tile_rows * (span_cols + 1))  67.9 us
    all_to_all x1, waiting for transfers between devices, to_tokens(): lax.all_to_all(ordered, 'dp', split_axis=0, concat_axis=0, tiled=True)  53.2 us
    dot_general x6, matrix products, times_transpose(): lax.dot_general(left, right, (((1,), (1,)), ((), ())), preferred_element_...  52.7 us
  transfers between devices with their start and end apart: 10, of which 4 were waited for; matrix products, arithmetic and copies ran while one was open for 57% of the time, Pallas kernels for 0%

commit v1 on v0

v1 whole, which is shorter than its diff:
```python
from functools import partial

import jax
import jax.numpy as jnp
from jax import lax
from jax.experimental import pallas as pl
from jax.experimental.pallas import tpu as pltpu
from jax.sharding import PartitionSpec as P

HDIM = 64
NBUCKET = 32
BLOCK = 256
LANES = 128
EPSILON = 1e-06
MASKED = -1e30
BF = jnp.bfloat16
F32 = jnp.float32
SPAN = 2 * BLOCK


def cost(micros):
    return pl.CostEstimate(flops=int(micros * 1.1e9), bytes_accessed=0, transcendentals=0)


def mm(left, right):
    return jnp.dot(left, right, preferred_element_type=F32)


def mm_t(left, right):
    return lax.dot_general(left, right, (((1,), (1,)), ((), ())), preferred_element_type=F32)


def one_hot(condition):
    return jnp.where(condition, 1.0, 0.0).astype(BF)


def rms_scale(values):
    return lax.rsqrt(jnp.mean(values * values, axis=-1, keepdims=True) + EPSILON)


def flip(values):
    return values.astype(F32).T.astype(BF)


def whole(kernel, outs, scratch, rank, arrays, micros, held=(), limit=56):
    vmem = pl.BlockSpec(memory_space=pltpu.VMEM)
    seen = 1 + len(arrays)

    def body(*refs):
        kernel(*refs[:seen], *refs[seen + len(held) :])

    return pl.pallas_call(
        body,
        out_shape=outs,
        in_specs=[pl.BlockSpec(memory_space=pltpu.SMEM)]
        + [vmem] * len(arrays)
        + [pl.BlockSpec(memory_space=pl.ANY)] * len(held),
        out_specs=[vmem] * len(outs),
        scratch_shapes=scratch,
        compiler_params=pltpu.CompilerParams(vmem_limit_bytes=limit * 1024 * 1024),
        cost_estimate=cost(micros),
    )(rank, *arrays, *held)


def idle_kernel(*refs):
    pass


def after(values, *others):
    anywhere = pl.BlockSpec(memory_space=pl.ANY)
    return pl.pallas_call(
        idle_kernel,
        out_shape=jax.ShapeDtypeStruct(values.shape, values.dtype),
        in_specs=[anywhere] * (1 + len(others)),
        out_specs=anywhere,
        input_output_aliases={0: 0},
    )(values, *others)


def shape(dims, kind):
    return jax.ShapeDtypeStruct(dims, kind)


def first_row(rank, shift, ranks, rows):
    return pl.multiple_of(lax.rem(rank + (shift + ranks), ranks) * rows, rows)


def wanted_slots(rank, slots, group):
    return (lax.broadcasted_iota(jnp.int32, (slots, group), 0) + rank * slots).astype(F32)


def route_kernel(slots, rank_ref, routes_ref, routes_t_ref, by_row_ref, by_col_ref, partner_ref):
    experts, group = by_row_ref.shape
    down = lax.broadcasted_iota(jnp.int32, (group, group), 0)
    across = lax.broadcasted_iota(jnp.int32, (group, group), 1)
    first, second = routes_t_ref[0:1, :], routes_t_ref[1:2, :]
    ids = lax.broadcasted_iota(jnp.int32, (experts, group), 0)
    named = (first == ids) | (second == ids)
    earlier = mm(one_hot(named), one_hot(down < across))
    by_row_ref[...] = jnp.where(named, earlier, -1.0)
    lane = lax.broadcasted_iota(jnp.int32, (group, LANES), 1)
    named_col = (routes_ref[:, 0:1] == lane) | (routes_ref[:, 1:2] == lane)
    earlier_col = mm(one_hot(across < down), one_hot(named_col))
    by_col_ref[...] = jnp.where(named_col, earlier_col, -1.0)
    pair = (first + second).astype(F32)
    wanted = wanted_slots(0, LANES, group) + (rank_ref[0] * slots).astype(F32)

    @pl.loop(0, experts)
    def _(expert):
        pick = one_hot(by_row_ref[pl.ds(expert, 1), :] == wanted)
        partner = jnp.broadcast_to(pair - expert.astype(F32) + 1.0, (16, group)).astype(BF)
        partner_ref[expert] = (mm_t(partner, pick) - 1.0).astype(BF)


def grad_rows_kernel(ranks, rank_ref, by_row_ref, *refs):
    pieces = refs[:ranks]
    rows_ref, grad_all = refs[ranks:]
    rank = rank_ref[0]
    group, own = grad_all.shape[0], pieces[0].shape[0]
    experts, slots, _ = rows_ref.shape
    for shift, piece in enumerate(pieces):
        grad_all[pl.ds(first_row(rank, -shift, ranks, own), own), :] = piece[...]
    wanted = wanted_slots(rank, slots, group)

    @pl.loop(0, experts)
    def _(expert):
        pick = one_hot(by_row_ref[pl.ds(expert, 1), :] == wanted)
        rows_ref[expert] = mm(pick, grad_all[...]).astype(BF)


def bias_tile(offsets, distance, seq_len):
    start = seq_len - BLOCK + BLOCK * distance
    spread = jnp.broadcast_to(offsets[:, start : start + SPAN], (BLOCK, SPAN))
    return pltpu.roll(spread, BLOCK, 1, stride=1, stride_axis=0)[:, :BLOCK]


def spread_heads(pair_t):
    head_row = lax.broadcasted_iota(jnp.int32, pair_t.shape, 0) < HDIM
    zero = jnp.zeros_like(pair_t)
    return jnp.where(head_row, pair_t, zero).astype(BF), jnp.where(head_row, zero, pair_t).astype(BF)


def attend_kernel(ranks, rank_ref, gain_ref, weight_ref, table_ref, buckets_ref, *refs):
    pieces = refs[:ranks]
    qkv_ref, attended_ref, log_ref, offsets_ref, bias = refs[ranks:]
    rank = rank_ref[0]
    own = pieces[0].shape[0]
    seq_len, heads_wide = attended_ref.shape
    tile = min(BLOCK, own)
    gain = gain_ref[...]
    for shift, piece in enumerate(pieces):
        base = first_row(rank, -shift, ranks, own)
        for row in range(0, own, tile):
            token_f = piece[row : row + tile, :].astype(F32)
            normed = (token_f * rms_scale(token_f) * gain).astype(BF)
            qkv_ref[pl.ds(base + row, tile), :] = mm(
                normed, weight_ref[:, : 3 * heads_wide]
            ).astype(BF)
    bucket = lax.broadcasted_iota(jnp.int32, (LANES, 2 * seq_len), 0)
    offsets_ref[...] = mm(table_ref[...], one_hot(bucket == buckets_ref[...]))
    blocks = seq_len // BLOCK

    @pl.loop(0, heads_wide // LANES)
    def _(pair):
        column = pl.multiple_of(pair * LANES, LANES)
        queries = spread_heads(
            (qkv_ref[:, pl.ds(column, LANES)].astype(F32) * 0.125).T
        )
        keys = qkv_ref[:, pl.ds(column + heads_wide, LANES)]
        values_t = flip(qkv_ref[:, pl.ds(column + 2 * heads_wide, LANES)])
        for head in range(2):
            for distance in range(blocks):
                bias[head, distance] = bias_tile(
                    offsets_ref[pl.ds(2 * pair + head, 1), :], distance, seq_len
                )
        for block in range(blocks):
            here = slice(block * BLOCK, (block + 1) * BLOCK)
            both = []
            for head in range(2):
                scores = []
                for other in range(block + 1):
                    there = slice(other * BLOCK, (other + 1) * BLOCK)
                    scores.append(mm(keys[there], queries[head][:, here]) + bias[head, block - other])
                top = jnp.max(scores[0], axis=0, keepdims=True)
                for part in scores[1:]:
                    top = jnp.maximum(top, jnp.max(part, axis=0, keepdims=True))
                total = jnp.zeros((1, BLOCK), F32)
                mixed = jnp.zeros((HDIM, BLOCK), F32)
                for other, part in enumerate(scores):
                    there = slice(other * BLOCK, (other + 1) * BLOCK)
                    exponent = jnp.exp(part - top)
                    total += jnp.sum(exponent, axis=0, keepdims=True)
                    mixed += mm(
                        values_t[head * HDIM : (head + 1) * HDIM, there], exponent.astype(BF)
                    )
                both.append(mixed / total)
                log_ref[pl.ds(2 * pair + head, 1), here] = top + jnp.log(total)
            attended_ref[here, pl.ds(column, LANES)] = jnp.concatenate(both, axis=0).T.astype(BF)


def post_kernel(ranks, chunks, rank_ref, gain_ref, by_row_ref, *refs):
    tokens = refs[:ranks]
    attended = refs[ranks : 2 * ranks]
    weights = refs[2 * ranks : 3 * ranks]
    mid_ref, *rows_refs = refs[3 * ranks : 3 * ranks + 1 + chunks]
    moe_in, turned = refs[3 * ranks + 1 + chunks :]
    rank = rank_ref[0]
    own = tokens[0].shape[0]
    tile = min(BLOCK, own)
    gain = gain_ref[...]
    for index, weight in enumerate(weights):
        turned[index] = flip(weight[...])
    for shift, piece in enumerate(tokens):
        base = first_row(rank, -shift, ranks, own)
        for row in range(0, own, tile):
            mid = piece[row : row + tile, :].astype(F32)
            for index, heads in enumerate(attended):
                mid = mid + mm(heads[pl.ds(base + row, tile), :], turned[index])
            if shift == 0:
                mid_ref[row : row + tile, :] = mid
            moe_in[pl.ds(base + row, tile), :] = (mid * rms_scale(mid) * gain).astype(BF)
    group = moe_in.shape[0]
    experts, slots, _ = rows_refs[0].shape
    wanted = wanted_slots(rank, slots * chunks, group)

    @pl.loop(0, experts)
    def _(expert):
        pick = one_hot(by_row_ref[pl.ds(expert, 1), :] == wanted)
        rows = mm(pick, moe_in[...]).astype(BF)
        for chunk, rows_ref in enumerate(rows_refs):
            rows_ref[expert] = rows[chunk * slots : (chunk + 1) * slots]


def gate_parts(own_id, experts, inputs, router, partner):
    lane = lax.broadcasted_iota(jnp.int32, (inputs.shape[0], LANES), 1)
    logits = jnp.where(lane < experts, mm(inputs, router), MASKED)
    exponent = jnp.exp(logits - jnp.max(logits, axis=-1, keepdims=True))
    probs = exponent / jnp.sum(exponent, axis=-1, keepdims=True)
    is_own, is_partner = lane == own_id, lane == partner
    chosen = jnp.sum(jnp.where(is_own, probs, 0.0), axis=-1, keepdims=True)
    pair = chosen + jnp.sum(jnp.where(is_partner, probs, 0.0), axis=-1, keepdims=True)
    return probs, is_own, is_partner, pair, chosen / pair


def gelu_parts(value):
    square = value * value
    slope = 0.7978845608028654
    curve = 0.7978845608028654 * 0.044715
    tanh = jnp.tanh(value * (slope + curve * square))
    half = 0.5 + 0.5 * tanh
    inner = value * (slope + 3.0 * curve * square)
    return value * half, half + half * (1.0 - tanh) * inner


def expert_kernel(
    steps, experts, first_slot, first, last, carried, ids_ref, rows_ref, grads_ref, partner_ref,
    router_ref, in_ref, in_t_ref, out_ref, out_t_ref, *refs
):
    if first:
        refs = refs[carried:]
        dpart_ref, kept_ref, act_ref, dpre_ref, *refs = refs
    else:
        given_result, given_din, dpart_ref, *refs = refs
        act_ref, dpre_ref, *refs = refs[carried:]
    if last:
        din_ref, route_grad_ref, result_ref, result_acc, din_acc = refs
    else:
        part_result_ref, part_din_ref, result_acc, din_acc = refs
    step = pl.program_id(0)
    own_id = ids_ref[0]
    sources, slots, width = rows_ref.shape
    total = sources * slots
    group = BLOCK // slots

    def group_parts(index):
        some = pl.ds(index * group, group)
        inputs = rows_ref[some].reshape(BLOCK, width)
        grad = grads_ref[some].reshape(BLOCK, width)
        row = lax.broadcasted_iota(jnp.int32, (BLOCK, LANES), 0) % slots + first_slot
        square = row == lax.broadcasted_iota(jnp.int32, (BLOCK, LANES), 1)
        spread = jnp.concatenate(
            [
                jnp.broadcast_to(
                    partner_ref[index * group + i][0:1].astype(F32),
                    (slots, LANES),
                )
                for i in range(group)
            ],
            axis=0,
        )
        partner = jnp.sum(jnp.where(square, spread, 0.0), axis=-1, keepdims=True).astype(jnp.int32)
        return inputs, grad.astype(F32), gate_parts(
            own_id, experts, inputs, router_ref[...], partner
        )

    @pl.when(step == 0)
    def _():
        @pl.loop(0, total // BLOCK)
        def _(index):
            here = pl.ds(pl.multiple_of(index * BLOCK, BLOCK), BLOCK)
            if first:
                inputs, grad, parts = group_parts(index)
                dpart_ref[here, :] = (parts[-1] * grad).astype(BF)
                kept_ref[here, :] = inputs
            result_acc[here, :] = jnp.zeros((BLOCK, width), F32)
            din_acc[here, :] = jnp.zeros((BLOCK, width), F32)

    if not first:
        share = given_result.shape[0]

        @pl.when(step < total // share)
        def _():
            mine = pl.ds(pl.multiple_of(step * share, share), share)
            result_acc[mine, :] += given_result[...].astype(F32)
            din_acc[mine, :] += given_din[...].astype(F32)

    tiles = [slice(row, row + BLOCK) for row in range(0, total, BLOCK)]
    inner = [slice(col, col + BLOCK) for col in range(0, in_ref.shape[2], BLOCK)]
    outer = [slice(col, col + BLOCK) for col in range(0, width, BLOCK)]

    def first_products(t, j):
        some = slice(t.start // slots, t.stop // slots)
        inputs = rows_ref[some].reshape(BLOCK, width)
        return mm(inputs, in_ref[0, :, j]), mm(dpart_ref[t, :], out_t_ref[0, :, j])

    def vector_work(t, j, pre, dact):
        act, slope = gelu_parts(pre)
        act_ref[0, t, j] = act.astype(BF)
        dpre_ref[0, t, j] = (dact * slope).astype(BF)

    def second_products(t, n):
        result_acc[t, n] += mm(act_ref[0, t, :], out_ref[0, :, n])
        din_acc[t, n] += mm(dpre_ref[0, t, :], in_t_ref[0, :, n])

    waiting, ready = None, []
    for t in tiles:
        for j in inner:
            products = first_products(t, j)
            if waiting is not None:
                vector_work(*waiting)
            waiting = (t, j, *products)
            if ready:
                second_products(*ready.pop(0))
        ready += [(t, n) for n in outer]
        while len(ready) > len(outer):
            second_products(*ready.pop(0))
    vector_work(*waiting)
    for item in ready:
        second_products(*item)

    if not last:

        @pl.when(step == steps - 1)
        def _():
            part_result_ref[...] = result_acc[...].astype(BF)
            part_din_ref[...] = din_acc[...].astype(BF)

        return

    @pl.when(step == steps - 1)
    def _():
        route_grad_ref[...] = jnp.zeros_like(route_grad_ref)

        @pl.loop(0, total // BLOCK)
        def _(index):
            here = pl.ds(pl.multiple_of(index * BLOCK, BLOCK), BLOCK)
            some = pl.ds(index * group, group)
            inputs, grad, (probs, is_own, is_partner, pair, gate) = group_parts(index)
            result = result_acc[here, :]
            result_ref[some] = (gate * result).astype(BF).reshape(group, slots, width)
            dgate = jnp.sum(result * grad, axis=-1, keepdims=True)
            shared = dgate * gate
            dprobs = jnp.where(is_own, (dgate - shared) / pair, 0.0) + jnp.where(
                is_partner, -shared / pair, 0.0
            )
            dlogits = probs * (dprobs - jnp.sum(dprobs * probs, axis=-1, keepdims=True))
            high = dlogits.astype(BF)
            din_ref[some] = (
                (din_acc[here, :] + mm_t(high, router_ref[...]))
                .astype(BF)
                .reshape(group, slots, width)
            )
            turned = dlogits.T[: route_grad_ref.shape[0], :]
            high = turned.astype(BF)
            low = (turned - high.astype(F32)).astype(BF)
            route_grad_ref[...] += mm(high, inputs) + mm(low, inputs)


def expert_call(
    ids, rows, grads, partners, router, weights, chunk, chunks, experts, pieces, span, kept, made,
    given, micros,
):
    sources, slots, width = rows.shape
    hidden = weights[0].shape[2]
    all_slots = chunks * slots
    block = min(768, hidden)
    per_piece = hidden // block
    start, stop = span
    first, last = start == 0, stop == pieces
    steps = per_piece * (stop - start)
    total = sources * slots
    route_rows = max(16, experts)

    def still(*dims):
        return pl.BlockSpec(dims, lambda i: (0,) * len(dims), pipeline_mode=pl.Buffered(1))

    def cols(i):
        return start + i // per_piece, 0, i % per_piece

    def lines(i):
        return start + i // per_piece, i % per_piece, 0

    wide = pl.BlockSpec((1, width, block), cols)
    tall = pl.BlockSpec((1, block, width), lines)
    mine = pl.BlockSpec((total, width), lambda i: (chunk, 0), pipeline_mode=pl.Buffered(1))
    columns = pl.BlockSpec((1, total, block), lambda i: (start + i // per_piece, chunk, i % per_piece))
    anywhere = pl.BlockSpec(memory_space=pl.ANY)
    stack = shape((chunks * total, width), BF)
    hidden_stack = shape((pieces, chunks * total, hidden), BF)
    if first:
        carried = [*kept, *made]
        operands = carried
        specs = [anywhere] * len(carried)
        outs, out_specs = [stack, stack, hidden_stack, hidden_stack], [mine, mine, columns, columns]
        aliases = {9 + i: i for i in range(len(carried))}
    else:
        carried = made
        operands = [*given[:2], kept[0], *carried]
        shares = min(steps, 2)
        share = pl.BlockSpec((total // shares, width), lambda i: (jnp.minimum(i, shares - 1), 0))
        specs = [share, share, mine] + [anywhere] * len(carried)
        outs, out_specs = [hidden_stack, hidden_stack], [columns, columns]
        aliases = {12 + i: i for i in range(len(carried))}
    if last:
        results = given[2] if len(given) > 2 else None
        if results is not None:
            carried = [*carried, results]
            operands = [*operands, results]
            specs = [*specs, anywhere]
            aliases[9 + len(operands) - 1] = len(outs) + 2
        outs += [
            shape((sources, slots, width), BF),
            shape((route_rows, width), F32),
            shape((sources, all_slots, width), BF),
        ]
        out_specs += [
            still(sources, slots, width),
            still(route_rows, width),
            pl.BlockSpec(
                (sources, slots, width), lambda i: (0, chunk, 0), pipeline_mode=pl.Buffered(1)
            ),
        ]
    else:
        outs += [shape((total, width), BF)] * 2
        out_specs += [still(total, width)] * 2
    found = pl.pallas_call(
        partial(
            expert_kernel, steps, experts, chunk * slots, first, last, len(carried)
        ),
        grid=(steps,),
        in_specs=[
            pl.BlockSpec(memory_space=pltpu.SMEM),
            still(sources, slots, width),
            pl.BlockSpec(
                (sources, slots, width), lambda i: (0, chunk, 0), pipeline_mode=pl.Buffered(1)
            ),
            still(*partners.shape),
            still(width, LANES),
            wide,
            tall,
            tall,
            wide,
        ]
        + specs,
        out_specs=out_specs,
        out_shape=outs,
        input_output_aliases=aliases,
        scratch_shapes=[pltpu.VMEM((total, width), F32), pltpu.VMEM((total, width), F32)],
        compiler_params=pltpu.CompilerParams(
            dimension_semantics=("arbitrary",), vmem_limit_bytes=60 * 1024 * 1024
        ),
        cost_estimate=cost(micros),
    )(ids, rows, grads, partners, router, *weights, *operands)
    if first:
        return found[:2], found[2:4], found[4:]
    return kept, found[:2], found[2:]


def lay_kernel(columns, parts, carried, *refs):
    plain_ref, turned_ref, *copies = refs[parts + carried :]
    if copies:
        lone_ref, *copies = copies
    start = 0
    for part in refs[:parts]:
        if columns:
            end = start + part.shape[1]
            plain_ref[0, :, start:end] = part[...]
            turned_ref[0, start:end, :] = part[...].T
        else:
            end = start + part.shape[0]
            plain_ref[0, start:end, :] = part[...]
            turned_ref[0, :, start:end] = part[...].T
        start = end
    if copies:
        lone_ref[0] = refs[0][...].T
    start = 0
    for copy in copies:
        if columns:
            copy[...] = refs[0][:, start : start + copy.shape[1]]
            start += copy.shape[1]
        else:
            copy[...] = refs[0][start : start + copy.shape[0], :]
            start += copy.shape[0]


def lay_call(ranks, piece, columns, parts, earlier, micros, lengths=()):
    axis = 1 if columns else 0
    rows, cols = parts[0].shape
    length = sum(part.shape[axis] for part in parts)
    runs = [(rows, run) if columns else (run, cols) for run in lengths]
    rows, cols = (rows, length) if columns else (length, cols)
    vmem = pl.BlockSpec(memory_space=pltpu.VMEM)
    return pl.pallas_call(
        partial(lay_kernel, columns, len(parts), len(earlier)),
        grid=(1,),
        in_specs=[vmem] * len(parts) + [pl.BlockSpec(memory_space=pl.ANY)] * len(earlier),
        out_specs=[
            pl.BlockSpec((1, rows, cols), lambda i: (piece, 0, 0), pipeline_mode=pl.Buffered(1)),
            pl.BlockSpec((1, cols, rows), lambda i: (piece, 0, 0), pipeline_mode=pl.Buffered(1)),
        ]
        + [vmem] * (len(runs) + (1 if runs else 0)),
        out_shape=[shape((ranks, rows, cols), BF), shape((ranks, cols, rows), BF)]
        + ([shape((1, cols, rows), BF)] if runs else [])
        + [shape(run, BF) for run in runs],
        input_output_aliases={len(parts) + i: i for i in range(len(earlier))},
        compiler_params=pltpu.CompilerParams(vmem_limit_bytes=60 * 1024 * 1024),
        cost_estimate=cost(micros),
    )(*parts, *earlier)


def add_kernel(pairs, own_ref, *refs):
    out_ref = refs[-1]
    for index in range(2):

        @pl.when(pl.program_id(0) == index)
        def _():
            total = own_ref[...]
            for pair in range(pairs):
                total = total + refs[2 * pair + index][...].astype(F32)
            out_ref[...] = total


def add_call(own, pairs):
    rows, cols = own.shape
    block = pl.BlockSpec((rows // 2, cols), lambda i: (i, 0))
    half = pl.BlockSpec(
        (rows // 2, cols), lambda i: (0, 0), pipeline_mode=pl.Buffered(1)
    )
    return pl.pallas_call(
        partial(add_kernel, len(pairs)),
        grid=(2,),
        in_specs=[block] + [half] * (2 * len(pairs)),
        out_specs=block,
        out_shape=shape(own.shape, F32),
        compiler_params=pltpu.CompilerParams(
            dimension_semantics=("arbitrary",), vmem_limit_bytes=40 * 1024 * 1024
        ),
        cost_estimate=cost(0),
    )(own, *[part for pair in pairs for part in pair])


def combine_kernel(ranks, chunks, rank_ref, by_col_ref, *refs):
    parts, (own_ref, other_ref, spread) = refs[:chunks], refs[chunks:]
    rank = rank_ref[0]
    own, _ = own_ref.shape
    experts, slots, width = parts[0].shape
    total = experts * slots
    tile = min(BLOCK, own)
    lane = lax.broadcasted_iota(jnp.int32, (LANES, total), 1)
    spread[...] = one_hot(lax.broadcasted_iota(jnp.int32, (LANES, total), 0) == lane // slots)
    slot = lax.broadcasted_iota(jnp.int32, (tile, total), 1) % slots + rank * (chunks * slots)
    wanted = slot.astype(F32)
    for shift in range(ranks):
        base = first_row(rank, shift, ranks, own)

        @pl.loop(0, own // tile)
        def _(index):
            row = pl.multiple_of(index * tile, tile)
            here = by_col_ref[pl.ds(base + row, tile), :].astype(BF)
            found = mm(here, spread[...]) - wanted
            part = jnp.zeros((tile, width), F32)
            for chunk, rows in enumerate(parts):
                pick = one_hot(found == float(chunk * slots))
                part = part + mm(pick, rows[...].reshape(total, width))
            if shift == 0:
                own_ref[pl.ds(row, tile), :] = part
            else:
                other_ref[shift - 1, pl.ds(row, tile), :] = part.astype(BF)


def combine_call(rank, ranks, by_col, parts, own, micros, held=()):
    experts, slots, width = parts[0].shape
    return whole(
        partial(combine_kernel, ranks, len(parts)),
        [shape((own, width), F32), shape((ranks - 1, own, width), BF)],
        [pltpu.VMEM((LANES, experts * slots), BF)],
        rank,
        [by_col, *parts],
        micros,
        held,
    )


def norm_back(values, scale, gain, upstream):
    normed = values * scale
    weighted = upstream * gain
    return scale * (weighted - normed * jnp.mean(weighted * normed, axis=-1, keepdims=True))


def mid_back_kernel(ranks, rank_ref, gain_ref, mid_ref, grad_ref, part_ref, *refs):
    received = refs[: ranks - 1]
    weights = refs[ranks - 1 : 2 * ranks - 1]
    dmid_ref, dbranch_ref, heads_ref, other_heads_ref, gain_grad_ref = refs[2 * ranks - 1 :]
    own = mid_ref.shape[0]
    tile = min(BLOCK, own)
    gain_grad = jnp.zeros(gain_ref.shape, F32)
    for row in range(0, own, tile):
        here = slice(row, row + tile)
        dmoe = part_ref[here, :]
        for piece in received:
            dmoe = dmoe + piece[here, :].astype(F32)
        mid = mid_ref[here, :]
        scale = rms_scale(mid)
        gain_grad += jnp.sum(dmoe * (mid * scale), axis=0, keepdims=True)
        dmid = grad_ref[here, :].astype(F32) + norm_back(mid, scale, gain_ref[...], dmoe)
        dmid_ref[here, :] = dmid
        dbranch = dmid.astype(BF)
        dbranch_ref[here, :] = dbranch
        heads_ref[here, :] = mm(dbranch, weights[0][...]).astype(BF)
        for shift in range(1, ranks):
            other_heads_ref[shift - 1, here, :] = mm(dbranch, weights[ranks - shift][...]).astype(
                BF
            )
    gain_grad_ref[...] = gain_grad


def diagonal_sums(tile):
    padded = jnp.concatenate([tile, jnp.zeros_like(tile)], axis=1)
    half = BLOCK // 2
    while half >= 8:
        padded = padded[:half] + pltpu.roll(padded[half:], SPAN - half, 1)
        half //= 2
    row = lax.broadcasted_iota(jnp.int32, padded.shape, 0)
    for bit in (4, 2, 1):
        padded = jnp.where((row & bit) != 0, pltpu.roll(padded, SPAN - bit, 1), padded)
    return pltpu.roll(jnp.sum(padded, axis=0, keepdims=True), BLOCK, 1)


def attend_back_kernel(
    ranks, head_count, rank_ref, qkv_ref, log_ref, offsets_ref, buckets_ref, *refs
):
    grad_pieces = refs[:ranks]
    dqkv, table_ref, bias, bias_grad, dattended, dkeys, dvalues, offset_grad = refs[ranks:]
    rank = rank_ref[0]
    own, heads_wide = grad_pieces[0].shape
    seq_len = dqkv.shape[0]
    blocks = seq_len // BLOCK
    for shift, piece in enumerate(grad_pieces):
        dattended[pl.ds(first_row(rank, -shift, ranks, own), own), :] = piece[...]
    offset_grad[...] = jnp.zeros_like(offset_grad)
    lane_head = lax.broadcasted_iota(jnp.int32, (1, LANES), 1) < HDIM

    @pl.loop(0, heads_wide // LANES)
    def _(pair):
        column = pl.multiple_of(pair * LANES, LANES)
        queries = (qkv_ref[:, pl.ds(column, LANES)].astype(F32) * 0.125).astype(BF)
        queries_t = spread_heads(queries.astype(F32).T)
        keys = qkv_ref[:, pl.ds(column + heads_wide, LANES)]
        keys_t = flip(keys)
        values = qkv_ref[:, pl.ds(column + 2 * heads_wide, LANES)]
        grads = dattended[:, pl.ds(column, LANES)]
        grads_t = spread_heads(grads.astype(F32).T)
        none = jnp.zeros_like(queries)
        queries_h = (jnp.where(lane_head, queries, none), jnp.where(lane_head, none, queries))
        grads_h = (jnp.where(lane_head, grads, none), jnp.where(lane_head, none, grads))
        for head in range(2):
            for distance in range(blocks):
                bias[head, distance] = bias_tile(
                    offsets_ref[pl.ds(2 * pair + head, 1), :], distance, seq_len
                )
        bias_grad[...] = jnp.zeros_like(bias_grad)
        dkeys[...] = jnp.zeros_like(dkeys)
        dvalues[...] = jnp.zeros_like(dvalues)
        for block in range(blocks):
            here = slice(block * BLOCK, (block + 1) * BLOCK)
            dqueries = []
            for head in range(2):
                log_row = log_ref[pl.ds(2 * pair + head, 1), here]
                weights, dweights = [], []
                overlap = jnp.zeros((1, BLOCK), F32)
                for other in range(block + 1):
                    there = slice(other * BLOCK, (other + 1) * BLOCK)
                    scores = mm(keys[there], queries_t[head][:, here]) + bias[head, block - other]
                    weight = jnp.exp(scores - log_row)
                    dweight = mm(values[there], grads_t[head][:, here])
                    overlap += jnp.sum(weight * dweight, axis=0, keepdims=True)
                    dvalues[there, :] += mm(weight.astype(BF), grads_h[head][here])
                    weights.append(weight)
                    dweights.append(dweight)
                dquery = jnp.zeros((HDIM, BLOCK), F32)
                for other in range(block + 1):
                    there = slice(other * BLOCK, (other + 1) * BLOCK)
                    dscores = weights[other] * (dweights[other] - overlap)
                    bias_grad[head, block - other] += dscores
                    dscores = dscores.astype(BF)
                    dkeys[there, :] += mm(dscores, queries_h[head][here])
                    dquery += mm(keys_t[head * HDIM : (head + 1) * HDIM, there], dscores)
                dqueries.append(dquery)
            dqkv[here, pl.ds(column, LANES)] = (
                jnp.concatenate(dqueries, axis=0).T * 0.125
            ).astype(BF)
        dqkv[:, pl.ds(column + heads_wide, LANES)] = dkeys[...].astype(BF)
        dqkv[:, pl.ds(column + 2 * heads_wide, LANES)] = dvalues[...].astype(BF)
        for head in range(2):
            for distance in range(blocks):
                start = seq_len - BLOCK + BLOCK * distance
                offset_grad[pl.ds(2 * pair + head, 1), start : start + SPAN] += diagonal_sums(
                    bias_grad[head, distance]
                )

    bucket = lax.broadcasted_iota(jnp.int32, (LANES, 2 * seq_len), 0)
    hot = one_hot(bucket == buckets_ref[...])
    high = offset_grad[...].astype(BF)
    rest = offset_grad[...] - high.astype(F32)
    low = rest.astype(BF)
    lowest = (rest - low.astype(F32)).astype(BF)
    table = mm_t(high, hot) + mm_t(low, hot) + mm_t(lowest, hot)
    row = lax.broadcasted_iota(jnp.int32, (16, LANES), 0) - rank * head_count
    placed = jnp.zeros((16, LANES), F32)
    for head in range(head_count):
        placed += jnp.where(row == head, table[head : head + 1, :], 0.0)
    table_ref[...] = placed


def project_grad_kernel(ranks, rank_ref, gain_ref, dqkv, dbranch_ref, *refs):
    tokens, attended_pieces = refs[:ranks], refs[ranks : 2 * ranks]
    grad_ref, normed_t = refs[2 * ranks :]
    rank = rank_ref[0]
    own, width = tokens[0].shape
    heads_wide = attended_pieces[0].shape[1]
    tile = min(BLOCK, own)
    for shift in range(ranks):
        base = first_row(rank, -shift, ranks, own)
        for row in range(0, own, tile):
            token_f = tokens[shift][row : row + tile, :].astype(F32)
            normed = token_f * rms_scale(token_f) * gain_ref[...]
            normed_t[:, pl.ds(base + row, tile)] = normed.T.astype(BF)
    here = pl.ds(first_row(rank, 0, ranks, own), own)
    for row in range(0, width, BLOCK):
        there = slice(row, row + BLOCK)
        grad_ref[there, : 3 * heads_wide] = mm(normed_t[there, :], dqkv[...]).astype(BF)
        dbranch_t = flip(dbranch_ref[:, there])
        for piece, attended in enumerate(attended_pieces):
            first = (3 + piece) * heads_wide
            grad_ref[there, first : first + heads_wide] = mm(dbranch_t, attended[here, :]).astype(BF)


def project_back_kernel(ranks, rank_ref, weight_ref, dqkv, table_ref, *refs):
    tokens = refs[:ranks]
    dnormed_ref, dnormed_other_ref, small_ref, gain_grad, dnormed_all = refs[ranks:]
    rank = rank_ref[0]
    own, width = tokens[0].shape
    columns = dqkv.shape[1]
    tile = min(BLOCK, own)
    gain_grad[...] = jnp.zeros_like(gain_grad)
    for row in range(0, width, BLOCK):
        there = slice(row, row + BLOCK)
        dnormed_all[:, there] = mm_t(dqkv[...], weight_ref[there, :columns])
    for shift in range(ranks):
        base = first_row(rank, -shift, ranks, own)
        for row in range(0, own, tile):
            token_f = tokens[shift][row : row + tile, :].astype(F32)
            plain = token_f * rms_scale(token_f)
            dnormed = dnormed_all[pl.ds(base + row, tile), :]
            gain_grad[...] += jnp.sum(dnormed * plain, axis=0, keepdims=True)
            if shift == 0:
                dnormed_ref[row : row + tile, :] = dnormed
            else:
                dnormed_other_ref[ranks - shift - 1, row : row + tile, :] = dnormed.astype(BF)
    small_ref[...] = jnp.zeros_like(small_ref)
    small_ref[0:1, :] = gain_grad[...]
    small_ref[8:24, 0:LANES] = table_ref[...]


def token_back_kernel(ranks, rank_ref, gain_ref, tokens_ref, dmid_ref, part_ref, *refs):
    received, out_ref = refs[: ranks - 1], refs[ranks - 1]
    own = tokens_ref.shape[0]
    tile = min(BLOCK, own)
    for row in range(0, own, tile):
        here = slice(row, row + tile)
        dnormed = part_ref[here, :]
        for piece in received:
            dnormed = dnormed + piece[here, :].astype(F32)
        token_f = tokens_ref[here, :].astype(F32)
        out_ref[here, :] = dmid_ref[here, :] + norm_back(
            token_f, rms_scale(token_f), gain_ref[...], dnormed
        )


def per_device(
    ranks, tokens, norm1_gain, qkv_weight, attn_out_weight, bias_table, buckets, norm2_gain,
    router_weight, routes, expert_in_weight, expert_out_weight, cotangent,
):
    rank = lax.axis_index("mp").astype(jnp.int32)
    rank_arr = rank.reshape(1)
    own, width = tokens.shape
    group = routes.shape[0]
    experts = router_weight.shape[1]
    slots = 4 * group // experts // ranks
    hidden = expert_in_weight.shape[2]
    heads_true = qkv_weight.shape[2]
    head_count = heads_true // HDIM
    heads_wide = -(-heads_true // LANES) * LANES
    head_rows = 16
    chunks = 2 if slots >= 32 else 1

    def sent(values, shift):
        return lax.ppermute(values, "mp", [(i, (i + shift) % ranks) for i in range(ranks)])

    def pieces(values):
        return [values] + [sent(values, shift) for shift in range(1, ranks)]

    def exchanged(parts):
        return [sent(parts[shift - 1], shift) for shift in range(1, ranks)]

    def to_experts(rows):
        return lax.all_to_all(rows, "dp", split_axis=0, concat_axis=0, tiled=True)

    def everywhere(values, late):
        for axis, size in (("dp", experts), ("mp", ranks)):
            if axis == "mp":
                values = after(values, *late)
            bit = 1
            while bit < size:
                others = range(bit, 4 * bit if 4 * bit <= size else 2 * bit, bit)
                values = values + sum(
                    lax.ppermute(values, axis, [(i, i ^ other) for i in range(size)])
                    for other in others
                )
                bit *= 1 + len(others)
        return values

    pad_heads = heads_wide - heads_true
    gain_one = norm1_gain.astype(F32).reshape(1, width)
    gain_two = norm2_gain.astype(F32).reshape(1, width)
    out_shard = jnp.pad(attn_out_weight.T, ((0, 0), (0, pad_heads)))
    shard = jnp.concatenate(
        [
            jnp.pad(qkv_weight, ((0, 0), (0, 0), (0, pad_heads))).reshape(-1, 3 * heads_wide),
            *pieces(out_shard),
        ],
        axis=1,
    )
    weights = lax.all_gather(shard, "dp", axis=0, tiled=True)
    out_pieces = [
        weights[:, (3 + piece) * heads_wide : (4 + piece) * heads_wide] for piece in range(ranks)
    ]
    grad_pieces = pieces(cotangent)
    token_pieces = pieces(tokens)
    in_own, out_own = expert_in_weight[0], expert_out_weight[0]
    quarter = hidden // 4
    *in_stacks, own_in_t, in_first, in_second, in_third = lay_call(
        ranks, 0, True, [in_own], [], 0, (quarter, 2 * quarter, quarter)
    )
    *out_stacks, own_out_t, out_whole = lay_call(ranks, 0, False, [out_own], [], 0, (hidden,))
    own_stacks = (expert_in_weight, own_in_t, expert_out_weight, own_out_t)
    in_first = pieces(after(in_first, *token_pieces[1:]))
    in_second = pieces(after(in_second, *in_first[1:]))
    table = lax.dynamic_slice_in_dim(bias_table.T, rank * head_count, head_count, 0)
    table = jnp.pad(table, ((0, head_rows - head_count), (0, LANES - NBUCKET)))
    lookup = jnp.concatenate([jnp.full((1,), -1, jnp.int32), buckets]).reshape(1, 2 * group)
    router = jnp.pad(router_weight, ((0, 0), (0, LANES - experts)))

    by_row, by_col, partners = whole(
        partial(route_kernel, slots),
        [shape((experts, group), F32), shape((group, LANES), F32), shape((experts, 16, LANES), BF)],
        [],
        rank_arr,
        [routes, routes.T],
        0,
    )
    partners = to_experts(partners)
    (grad_rows,) = whole(
        partial(grad_rows_kernel, ranks),
        [shape((experts, slots, width), BF)],
        [pltpu.VMEM((group, width), BF)],
        rank_arr,
        [by_row, *grad_pieces],
        9,
        held=[partners, *token_pieces[1:], *in_stacks, *out_stacks],
    )
    grad_rows = to_experts(after(grad_rows, weights, *in_first[1:]))

    qkv, attended, log_sums, offsets = whole(
        partial(attend_kernel, ranks),
        [
            shape((group, 3 * heads_wide), BF),
            shape((group, heads_wide), BF),
            shape((8, group), F32),
            shape((head_rows, 2 * group), F32),
        ],
        [pltpu.VMEM((2, group // BLOCK, BLOCK, BLOCK), F32)],
        rank_arr,
        [gain_one, weights, table, lookup, *token_pieces],
        16,
    )
    attended_pieces = [attended] + pieces(after(attended, *in_second[1:]))[1:]
    in_third = pieces(after(in_third, *attended_pieces[1:]))
    out_whole = pieces(after(out_whole, *in_third[1:]))
    mid, *send_rows = whole(
        partial(post_kernel, ranks, chunks),
        [shape((own, width), F32)] + [shape((experts, slots // chunks, width), BF)] * chunks,
        [pltpu.VMEM((group, width), BF), pltpu.VMEM((ranks, heads_wide, width), BF)],
        rank_arr,
        [gain_two, by_row, *token_pieces, *attended_pieces, *out_pieces],
        12,
    )
    for piece in range(1, ranks):
        in_parts = [in_first[piece], in_second[piece], in_third[piece]]
        in_stacks = lay_call(ranks, piece, True, in_parts, in_stacks, 4)
    expert_rows = [to_experts(after(send_rows[0], grad_rows, *in_third[1:]))]
    for rows in send_rows[1:]:
        expert_rows.append(to_experts(after(rows, *expert_rows, *in_stacks)))
    own_expert = lax.axis_index("dp").astype(jnp.int32).reshape(1)
    kept, made, results, din_rows = [], [], [], []
    route_grad = jnp.zeros((max(16, experts), width), F32)
    for chunk in range(chunks):
        spans = [(0, 1), (1, ranks)] if chunk == 0 and ranks > 1 else [(0, ranks)]
        sums = []
        for span in spans:
            if span[1] == ranks:
                sums = [*(sums or [None, None]), *results]
            if span[0] == 1:
                for piece in range(1, ranks):
                    arrived = after(out_whole[piece], *sums[:2])
                    out_stacks = lay_call(ranks, piece, False, [arrived], out_stacks, 4)
            stacks = own_stacks if span == (0, 1) else (*in_stacks, *out_stacks)
            kept, made, sums = expert_call(
                own_expert, expert_rows[chunk], grad_rows, partners, router, stacks, chunk,
                chunks, experts, ranks, span, kept, made, sums, 4 if len(spans) > 1 else 35,
            )
        din, route_part, *results = sums
        din_rows.append(to_experts(din))
        route_grad = route_grad + route_part
    (dpart, rows_kept), (act, dpre) = kept, made
    (results,) = results

    def rows_dot(left, right):
        return lax.dot_general(left, right, (((0,), (0,)), ((), ())), preferred_element_type=F32)

    upper = [
        rows_dot(rows_kept[:, : width // 2], dpre[j]).astype(BF) for j in range(1, ranks)
    ]
    lower = [
        rows_dot(rows_kept[:, width // 2 :], dpre[j]).astype(BF) for j in range(1, ranks)
    ]
    out_grads = [rows_dot(act[j], dpart).astype(BF) for j in range(1, ranks)]
    firsts = [sent(grad, ranks - 1 - j) for j, grad in enumerate(upper)]
    seconds = [
        sent(after(grad, *firsts), ranks - 1 - j) for j, grad in enumerate(lower)
    ]
    dmoe_own, dmoe_other = combine_call(
        rank_arr, ranks, by_col, din_rows, own, 8, held=[*firsts, *out_grads]
    )
    dmoe_pieces = exchanged(dmoe_other)
    in_own_grad = rows_dot(after(rows_kept, dmoe_own), dpre[0])
    out_own_grad = rows_dot(act[0], after(dpart, dmoe_own))
    dmid, dbranch, dheads, other_dheads, gain_two_grad = whole(
        partial(mid_back_kernel, ranks),
        [
            shape((own, width), F32),
            shape((own, width), BF),
            shape((own, heads_wide), BF),
            shape((ranks - 1, own, heads_wide), BF),
            shape((1, width), F32),
        ],
        [],
        rank_arr,
        [gain_two, mid, cotangent, dmoe_own, *dmoe_pieces, *out_pieces],
        6,
        held=seconds,
    )
    dheads = [dheads, *exchanged(other_dheads)]
    thirds = [
        sent(after(grad[: hidden // 2], *dheads[1:]), ranks - 1 - j)
        for j, grad in enumerate(out_grads)
    ]
    early = jnp.concatenate([jnp.pad(gain_two_grad, ((0, 7), (0, 0))), route_grad], axis=0)
    results = to_experts(after(results, *firsts))

    dqkv, table_grad = whole(
        partial(attend_back_kernel, ranks, head_count),
        [shape((group, 3 * heads_wide), BF), shape((16, LANES), F32)],
        [
            pltpu.VMEM((2, group // BLOCK, BLOCK, BLOCK), F32),
            pltpu.VMEM((2, group // BLOCK, BLOCK, BLOCK), F32),
            pltpu.VMEM((group, heads_wide), BF),
            pltpu.VMEM((group, LANES), F32),
            pltpu.VMEM((group, LANES), F32),
            pltpu.VMEM((head_rows, 2 * group), F32),
        ],
        rank_arr,
        [qkv, log_sums, offsets, lookup, *dheads],
        20,
        held=[in_own_grad, out_own_grad],
    )
    (weight_grad,) = whole(
        partial(project_grad_kernel, ranks),
        [shape((width, (3 + ranks) * heads_wide), BF)],
        [pltpu.VMEM((width, group), BF)],
        rank_arr,
        [gain_one, dqkv, dbranch, *token_pieces, *attended_pieces],
        8,
        held=[results, *thirds],
    )
    core = lax.axis_index("dp") % 2
    shards = weight_grad.reshape(experts // 2, 2, width // experts, -1)
    swapped = lax.ppermute(
        lax.dynamic_index_in_dim(shards, 1 - core, 1, keepdims=False),
        "dp",
        [(i, i ^ 1) for i in range(experts)],
    )
    shards = lax.dynamic_index_in_dim(shards, core, 1, keepdims=False)
    shards = (shards.astype(F32) + swapped.astype(F32)).astype(BF)
    dnormed_own, dnormed_other, small = whole(
        partial(project_back_kernel, ranks),
        [
            shape((own, width), F32),
            shape((ranks - 1, own, width), BF),
            shape((24, width), F32),
        ],
        [pltpu.VMEM((1, width), F32), pltpu.VMEM((group, width), F32)],
        rank_arr,
        [weights, dqkv, table_grad, *token_pieces],
        7,
        held=[weight_grad],
    )
    dnormed_pieces = exchanged(after(dnormed_other, swapped))
    fourths = [
        sent(after(grad[hidden // 2 :], *dnormed_pieces), ranks - 1 - j)
        for j, grad in enumerate(out_grads)
    ]
    shards = lax.all_to_all(
        shards,
        "dp",
        split_axis=0,
        concat_axis=0,
        tiled=True,
        axis_index_groups=[list(range(start, experts, 2)) for start in range(2)],
    )
    (grad_tokens,) = whole(
        partial(token_back_kernel, ranks),
        [shape((own, width), F32)],
        [],
        rank_arr,
        [gain_one, tokens, dmid, dnormed_own, *dnormed_pieces],
        0,
    )

    weight_total = jnp.sum(shards.astype(F32), axis=0)
    qkv_grad = weight_total[:, : 3 * heads_wide].reshape(-1, 3, heads_wide)[:, :, :heads_true]
    out_part = jnp.split(weight_total[:, 3 * heads_wide :], ranks, axis=1)
    attn_out_grad = out_part[0]
    for shift in range(1, ranks):
        attn_out_grad = attn_out_grad + sent(out_part[shift], ranks - shift)
    attn_out_grad = attn_out_grad[:, :heads_true].T

    moe_own, moe_other = combine_call(
        rank_arr, ranks, by_col, [results], own, 0, held=dnormed_pieces
    )
    small = jnp.concatenate([small, early], axis=0)
    moe_pieces = exchanged(moe_other)
    small = everywhere(after(small, moe_own), [*moe_pieces, *fourths])
    mixed = mid + moe_own
    for piece in moe_pieces:
        mixed = mixed + piece.astype(F32)

    in_grad = add_call(in_own_grad, list(zip(firsts, seconds)))
    out_grad = add_call(out_own_grad, list(zip(thirds, fourths)))
    return (
        mixed.astype(BF),
        grad_tokens,
        small[0],
        qkv_grad,
        attn_out_grad,
        small[8 : 8 + bias_table.shape[1], :NBUCKET].T,
        small[24],
        small[32 : 32 + experts].T,
        in_grad[None],
        out_grad[None],
    )


def solution(mesh):
    placed = (
        P(("dp", "mp"), None),
        P(),
        P("dp", None, "mp"),
        P("mp", "dp"),
        P(),
        P(),
        P(),
        P(),
        P("dp", None),
        P("dp", None, "mp"),
        P("dp", "mp", None),
        P(("dp", "mp"), None),
    )
    return jax.shard_map(
        partial(per_device, mesh.shape["mp"]),
        mesh=mesh,
        in_specs=placed,
        out_specs=(
            P(("dp", "mp"), None),
            P(("dp", "mp"), None),
            P(),
            P("dp", None, "mp"),
            P("mp", "dp"),
            P(),
            P(),
            P(),
            P("dp", None, "mp"),
            P("dp", "mp", None),
        ),
        check_vma=False,
    )
```

time: 2360 us -> 527 us (0.22)
  local copies, waits for them, and re-layouts: 1280 us -> 36.8 us
  blocking collectives: 522 us -> 0 us
  Pallas kernels: 0 us -> 211 us
  matrix products: 196 us -> 32.9 us
  other arithmetic: 129 us -> 13.3 us
  starting transfers between devices: 6.06 us -> 88.6 us
  waiting for transfers between devices: 187 us -> 124 us
    unnamed x180 -> x87, local copies, waits for them, and re-layouts: 1010 us -> 24.3 us
    all_to_all x3 -> x0, blocking collectives: 452 us -> none  [the longest x2 309 us: to_experts(): lax.all_to_all(buffer, 'dp', split_axis=0, concat_axis=0, tiled=True)]
    pallas_call x0 -> x38, Pallas kernels: none -> 211 us  [the longest x11 107 us: whole(): pl.pallas_call(body, out_shape=outs, in_specs=[pl.BlockSpec(memory_space=...]
    dot_general x35 -> x5, matrix products: 196 us -> 32.9 us  [rows_dot(): lax.dot_general(left, right, (((0,), (0,)), ((), ())), preferred_element_...]
    psum x2 -> x0, waiting for transfers between devices: 104 us -> none  [the longest x1 68.4 us: per_device(): mid_all = lax.psum(with_tokens, 'mp')]
    ppermute x0 -> x25, waiting for transfers between devices: none -> 97.7 us  [the longest x17 85.3 us: sent(): lax.ppermute(values, 'mp', [(i, (i + shift) % ranks) for i in range(ranks)])]
    gather x5 -> x0, local copies, waits for them, and re-layouts: 93.6 us -> none  [the longest x2 27.3 us: to_tokens(): back.reshape(expert_total * capacity, width)[slot_index].astype(jnp.float32)]
    reshape x3 -> x4, local copies, waits for them, and re-layouts: 67.9 us -> 2.77 us  [the longest x1 0.91 us: per_device(): jnp.pad(qkv_weight, ((0, 0), (0, 0), (0, pad_heads)))]
  transfers between devices with their start and end apart: 10 -> 34, of which waited for: 4 -> 17; matrix products, arithmetic and copies ran while one was open for 57% -> 11% of each run, Pallas kernels for 0% -> 39%
where the time goes in v1:
time: 527 us; the launch traced here: 521 us
  Pallas kernels  211 us (40%)
  waiting for transfers between devices  124 us (24%)
  starting transfers between devices  88.6 us (17%)
  local copies, waits for them, and re-layouts  36.8 us (7%)
  matrix products  32.9 us (6%)
  between operations  15 us (3%)
  other arithmetic  13.3 us (3%)
    pallas_call x11, Pallas kernels, whole(): pl.pallas_call(body, out_shape=outs, in_specs=[pl.BlockSpec(memory_space=...  107 us
    ppermute x17, waiting for transfers between devices, sent(): lax.ppermute(values, 'mp', [(i, (i + shift) % ranks) for i in range(ranks)])  85.3 us
    pallas_call x3, Pallas kernels, expert_call(): pl.pallas_call(partial(expert_kernel, steps, experts, chunk * slots, firs...  78.1 us
    all_to_all x7, starting transfers between devices, to_experts(): return lax.all_to_all(rows, 'dp', split_axis=0, concat_axis=0, tiled=True)  52.1 us
    dot_general x5, matrix products, rows_dot(): lax.dot_general(left, right, (((0,), (0,)), ((), ())), preferred_element_...  32.9 us
    all_to_all x7, waiting for transfers between devices, to_experts(): return lax.all_to_all(rows, 'dp', split_axis=0, concat_axis=0, tiled=True)  25.9 us
    unnamed x87, local copies, waits for them, and re-layouts  24.3 us
    ppermute x17, starting transfers between devices, sent(): lax.ppermute(values, 'mp', [(i, (i + shift) % ranks) for i in range(ranks)])  23.3 us
  transfers between devices with their start and end apart: 34, of which 17 were waited for; matrix products, arithmetic and copies ran while one was open for 11% of the time, Pallas kernels for 39%

profile of v1, /device:TPU:0, one launch (start us, length us, event | category | flops | bytes accessed | tf_op | source)
XLA Modules:
  0.0 520.9 jit_solution(15647750840415303772)
XLA Ops:
  44.1 7.4 %collective-permute-done.5.refs_3_ = bf16[512,768]{1,0:T(8,128)(2,1)S(1)} collective-permute-done((bf16[512,768]{1,0:T(8,128)(2,1)}, bf16[512,768]{1,0:T(8,128)(2,1)S(1)}, u32[]{:S(2)}, u32[]{:S(2)}) %collective-permute-start.5) | collective-permute-done | bytes 786464 | tf_op jit(solution)/shard_map/ppermute | solution.py:828
  52.4 9.3 %shard_map.203.refs_0_ = bf16[16,128,768]{2,1,0:T(8,128)(2,1)} custom-call(s32[1]{0:T(128)} %bitcast.refs_0_, f32[16,1024]{1,0:T(8,128)} %get-tuple-element.66.refs_2_.refs_1_, bf16[512,768]{1,0:T(8,128)(2,1)} %refs_3_.3, bf16[512,768]{1,0:T(8,128)(2,1)} %copy-done.36, bf16[16,16,128]{2,1,0:T(8,128)(2,1)} %copy-done.27, bf16[512,768]{1,0:T(8,128)(2,1)} %copy-done.25, ...), custom_call_target="tpu_custom_call" | custom-call | flops 9900000256 | tf_op jit(solution)/shard_map/pallas_call | solution.py:52
  72.8 16.4 %shard_map.196 = (bf16[1024,1152]{1,0:T(8,128)(2,1)}, bf16[1024,384]{1,0:T(8,128)(2,1)}, f32[8,1024]{1,0:T(8,128)}, f32[16,2048]{1,0:T(8,128)}) custom-call(s32[1]{0:T(128)} %bitcast.refs_0_, f32[1,768]{1,0:T(1,128)} %reshape.63.refs_1_, bf16[768,1920]{1,0:T(8,128)(2,1)} %all-gather.2.cloned.1.call-done.refs_2_.refs_1_, bf16[16,128]{1,0:T(8,128)(2,1)} %pad.12.refs_3_, ...), custom_call_target="tpu_custom_call" | custom-call | flops 17600000000 | tf_op jit(solution)/shard_map/pallas_call | solution.py:52
  91.3 8.7 %collective-permute-done.3.refs_1_ = bf16[768,768]{1,0:T(8,128)(2,1)} collective-permute-done((bf16[768,768]{1,0:T(8,128)(2,1)}, bf16[768,768]{1,0:T(8,128)(2,1)}, u32[]{:S(2)}, u32[]{:S(2)}) %collective-permute-start.3) | collective-permute-done | bytes 1179680 | tf_op jit(solution)/shard_map/ppermute | solution.py:828
  104.5 15.0 %collective-permute-done.4.refs_6_.refs_1_.refs_7_ = bf16[1024,384]{1,0:T(8,128)(2,1)} collective-permute-done((bf16[1024,384]{1,0:T(8,128)(2,1)}, bf16[1024,384]{1,0:T(8,128)(2,1)}, u32[]{:S(2)}, u32[]{:S(2)}) %collective-permute-start.4) | collective-permute-done | bytes 786464 | tf_op jit(solution)/shard_map/ppermute | solution.py:828
  121.0 12.3 %shard_map.201 = (f32[512,768]{1,0:T(8,128)}, bf16[16,64,768]{2,1,0:T(8,128)(2,1)}, bf16[16,64,768]{2,1,0:T(8,128)(2,1)}) custom-call(s32[1]{0:T(128)} %bitcast.refs_0_, f32[1,768]{1,0:T(1,128)} %reshape.61.refs_1_, f32[16,1024]{1,0:T(8,128)} %get-tuple-element.66.refs_2_.refs_1_, bf16[512,768]{1,0:T(8,128)(2,1)} %refs_2_.3, bf16[512,768]{1,0:T(8,128)(2,1)} %copy-done.25, ...), custom_call_target="tpu_custom_call" | custom-call | flops 13200000000 | tf_op jit(solution)/shard_map/pallas_call | solution.py:52
  135.5 10.3 %all-to-all-start.2 = ((bf16[16,64,768]{2,1,0:T(8,128)(2,1)}), bf16[16,64,768]{2,1,0:T(8,128)(2,1)S(1)}, u32[]{:S(2)}, u32[]{:S(2)}) async-start(bf16[16,64,768]{2,1,0:T(8,128)(2,1)} %shard_map.206), calls=%async_computation.2 | async-start | bytes 3145728 | tf_op jit(solution)/shard_map/all_to_all | solution.py:837
  151.9 25.9 %all-to-all-done.2.refs_1_.rows_ref = bf16[16,64,768]{2,1,0:T(8,128)(2,1)S(1)} async-done(((bf16[16,64,768]{2,1,0:T(8,128)(2,1)}), bf16[16,64,768]{2,1,0:T(8,128)(2,1)S(1)}, u32[]{:S(2)}, u32[]{:S(2)}) %all-to-all-start.2) | async-done | bytes 1572896 | tf_op jit(solution)/shard_map/all_to_all | solution.py:837
  179.0 9.5 %all-to-all-start.3 = ((bf16[16,64,768]{2,1,0:T(8,128)(2,1)}), bf16[16,64,768]{2,1,0:T(8,128)(2,1)S(1)}, u32[]{:S(2)}, u32[]{:S(2)}) async-start(bf16[16,64,768]{2,1,0:T(8,128)(2,1)} %shard_map.208), calls=%async_computation.3 | async-start | bytes 3145728 | tf_op jit(solution)/shard_map/all_to_all | solution.py:837
  189.4 20.5 %shard_map.210 = (bf16[2048,768]{1,0:T(8,128)(2,1)}, bf16[2048,768]{1,0:T(8,128)(2,1)}, bf16[2,2048,1536]{2,1,0:T(8,128)(2,1)}, bf16[2,2048,1536]{2,1,0:T(8,128)...) custom-call(s32[1]{0:T(128)} %bitcast.6.ids_ref, bf16[16,64,768]{2,1,0:T(8,128)(2,1)} %copy-done.13, ...), custom_call_target="tpu_custom_call" | custom-call | flops 4400000000 | tf_op jit(solution)/shard_map/pallas_call | solution.py:456
  214.5 22.8 %shard_map.213 = (bf16[2,2048,1536]{2,1,0:T(8,128)(2,1)}, bf16[2,2048,1536]{2,1,0:T(8,128)(2,1)}, bf16[16,64,768]{2,1,0:T(8,128)(2,1)}, f32[16,768]{1,0:T(8,128)}, bf16[16,128,768]{2,1,0:T(8,128)(2,1)}) custom-call(s32[1]{0:T(128)} %bitcast.6.ids_ref, bf16[16,64,768]{2,1,0:T(8,128)(2,1)} %copy-done.13, ...), custom_call_target="tpu_custom_call", output_to_operand_aliasing={{0}: (12, {}), {1}: (13, {})} | custom-call | flops 4400000000 | tf_op jit(solution)/shard_map/pallas_call | solution.py:456
  237.3 6.7 %all-to-all-start.5 = ((bf16[16,64,768]{2,1,0:T(8,128)(2,1)}), bf16[16,64,768]{2,1,0:T(8,128)(2,1)}, u32[]{:S(2)}, u32[]{:S(2)}) async-start(bf16[16,64,768]{2,1,0:T(8,128)(2,1)} %get-tuple-element.102), calls=%async_computation.5 | async-start | bytes 3145728 | tf_op jit(solution)/shard_map/all_to_all | solution.py:837
  244.0 34.8 %shard_map.214 = (bf16[2048,768]{1,0:T(8,128)(2,1)}, bf16[2048,768]{1,0:T(8,128)(2,1)}, bf16[2,2048,1536]{2,1,0:T(8,128)(2,1)}, bf16[2,2048,1536]{2,1,0:T(8,128)...) custom-call(s32[1]{0:T(128)} %bitcast.6.ids_ref, ...), custom_call_target="tpu_custom_call", output_to_operand_aliasing={{0}: (9, {}), {1}: (10, {}), {2}: (11, {}), {3}: (12, {}), ... | custom-call | flops 38499999744 | tf_op jit(solution)/shard_map/pallas_call | solution.py:456
  278.8 6.7 %all-to-all-start.6 = ((bf16[16,64,768]{2,1,0:T(8,128)(2,1)}), bf16[16,64,768]{2,1,0:T(8,128)(2,1)}, u32[]{:S(2)}, u32[]{:S(2)}) async-start(bf16[16,64,768]{2,1,0:T(8,128)(2,1)} %get-tuple-element.103), calls=%async_computation.6 | async-start | bytes 3145728 | tf_op jit(solution)/shard_map/all_to_all | solution.py:837
  305.5 14.0 %collective-permute-done.8.refs_1_.refs_4_.refs_0_ = bf16[384,1536]{1,0:T(8,128)(2,1)S(1)} collective-permute-done((bf16[384,1536]{1,0:T(8,128)(2,1)S(1)}, bf16[384,1536]{1,0:T(8,128)(2,1)S(1)}, u32[]{:S(2)}, u32[]{:S(2)}) %collective-permute-start.8) | collective-permute-done | bytes 1179680 | tf_op jit(solution)/shard_map/ppermute | solution.py:828
  328.1 8.1 %shard_map.216 = (f32[512,768]{1,0:T(8,128)}, bf16[1,512,768]{2,1,0:T(8,128)(2,1)}) custom-call(s32[1]{0:T(128)} %bitcast.refs_0_, f32[1024,128]{1,0:T(8,128)} %get-tuple-element.71.refs_1_, bf16[16,64,768]{2,1,0:T(8,128)(2,1)} %all-to-all-done.5.refs_2_, bf16[16,64,768]{2,1,0:T(8,128)(2,1)} %all-to-all-done.6.refs_3_, bf16[384,1536]{1,0:T(8,128)(2,1)} %copy-done.2, ...), custom_call_target="tpu_custom_call" | custom-call | flops 8800000000 | tf_op jit(solution)/shard_map/pallas_call | solution.py:52
  337.9 9.6 %fusion.2.refs_7_.own_ref = f32[768,1536]{1,0:T(8,128)} fusion(bf16[2048,768]{1,0:T(8,128)(2,1)} %shard_map.219, bf16[2,2048,1536]{2,1,0:T(8,128)(2,1)} %get-tuple-element.98), kind=kOutput, calls=%fused_computation.2 | convolution fusion | flops 4831838208 | bytes 14155776 | tf_op jit(solution)/shard_map/dot_general | solution.py:959
  349.7 15.6 %collective-permute-done.9.refs_5_ = bf16[512,768]{1,0:T(8,128)(2,1)S(1)} collective-permute-done((bf16[512,768]{1,0:T(8,128)(2,1)S(1)}, bf16[512,768]{1,0:T(8,128)(2,1)S(1)}, u32[]{:S(2)}, u32[]{:S(2)}) %collective-permute-start.9) | collective-permute-done | bytes 786464 | tf_op jit(solution)/shard_map/ppermute | solution.py:828
  373.2 8.7 %fusion.refs_8_.own_ref = f32[1536,768]{1,0:T(8,128)} fusion(bf16[2048,768]{1,0:T(8,128)(2,1)S(1)} %copy-done.15, bf16[2,2048,1536]{2,1,0:T(8,128)(2,1)} %get-tuple-element.104), kind=kOutput, calls=%fused_computation | convolution fusion | flops 4831838208 | bytes 14155776 | tf_op jit(solution)/shard_map/dot_general | solution.py:959
  384.1 21.2 %shard_map.221 = (bf16[1024,1152]{1,0:T(8,128)(2,1)}, f32[16,128]{1,0:T(8,128)}) custom-call(s32[1]{0:T(128)} %bitcast.refs_0_, bf16[1024,1152]{1,0:T(8,128)(2,1)} %get-tuple-element.99.refs_1_, f32[8,1024]{1,0:T(8,128)} %get-tuple-element.100.refs_2_, f32[16,2048]{1,0:T(8,128)} %get-tuple-element.101.refs_3_, s32[1,2048]{1,0:T(1,128)} %bitcast.75, ...), custom_call_target="tpu_custom_call" | custom-call | flops 22000001024 | tf_op jit(solution)/shard_map/pallas_call | solution.py:52
  410.5 8.1 %shard_map.223.refs_6_ = bf16[768,1920]{1,0:T(8,128)(2,1)} custom-call(s32[1]{0:T(128)} %bitcast.refs_0_, f32[1,768]{1,0:T(1,128)} %reshape.63.refs_1_, bf16[1024,1152]{1,0:T(8,128)(2,1)} %get-tuple-element.110.refs_2_, bf16[512,768]{1,0:T(8,128)(2,1)} %get-tuple-element.112.refs_3_, bf16[512,768]{1,0:T(8,128)(2,1)} %refs_2_.3, bf16[512,768]{1,0:T(8,128)(2,1)} %copy-done.25, ...), custom_call_target="tpu_custom_call" | custom-call | flops 8800000000 | tf_op jit(solution)/shard_map/pallas_call | solution.py:52
  421.2 7.3 %shard_map.224 = (f32[512,768]{1,0:T(8,128)}, bf16[1,512,768]{2,1,0:T(8,128)(2,1)}, f32[24,768]{1,0:T(8,128)}) custom-call(s32[1]{0:T(128)} %bitcast.refs_0_, bf16[768,1920]{1,0:T(8,128)(2,1)} %all-gather.2.cloned.1.call-done.refs_2_.refs_1_, bf16[1024,1152]{1,0:T(8,128)(2,1)} %get-tuple-element.110.refs_2_, f32[16,128]{1,0:T(8,128)} %get-tuple-element.111.refs_3_, ...), custom_call_target="tpu_custom_call" | custom-call | flops 7699999744 | tf_op jit(solution)/shard_map/pallas_call | solution.py:52
  439.2 10.7 %collective-permute-done.14.refs_3_.refs_5_.refs_1_ = bf16[512,768]{1,0:T(8,128)(2,1)S(1)} collective-permute-done((bf16[512,768]{1,0:T(8,128)(2,1)}, bf16[512,768]{1,0:T(8,128)(2,1)S(1)}, u32[]{:S(2)}, u32[]{:S(2)}) %collective-permute-start.14) | collective-permute-done | bytes 786464 | tf_op jit(solution)/shard_map/ppermute | solution.py:828
  451.7 8.6 %shard_map.226 = (f32[512,768]{1,0:T(8,128)}, bf16[1,512,768]{2,1,0:T(8,128)(2,1)}) custom-call(s32[1]{0:T(128)} %bitcast.refs_0_, f32[1024,128]{1,0:T(8,128)} %get-tuple-element.71.refs_1_, bf16[16,128,768]{2,1,0:T(8,128)(2,1)} %all-to-all-done.4.refs_8_.refs_2_, bf16[512,768]{1,0:T(8,128)(2,1)} %copy-done.17), custom_call_target="tpu_custom_call" | custom-call | tf_op jit(solution)/shard_map/pallas_call | solution.py:52
  (202 shorter events, 187.7 us)
Async XLA Ops:
  7.2 54.9 %all-gather.2.cloned.1.call-start = ((), (), s32[]{:S(2)}) async-start(), calls=%async_computation.8 | async-start | bytes 3133440 | tf_op jit(solution)/shard_map/all_gather | solution.py:864
  13.9 27.9 %collective-permute-start = (bf16[512,768]{1,0:T(8,128)(2,1)}, bf16[512,768]{1,0:T(8,128)(2,1)S(1)}, u32[]{:S(2)}, u32[]{:S(2)}) collective-permute-start(bf16[512,768]{1,0:T(8,128)(2,1)} %refs_2_.3), channel_id=1, source_target_pairs={{0,1},{1,0},{2,3},{3,2},{4,5},{5,4},{6,7},{7,6},{8,9},{9,8},{10,11... | collective-permute-start | bytes 2359304 | tf_op jit(solution)/shard_map/ppermute | solution.py:828
  16.0 35.5 %collective-permute-start.5 = (bf16[512,768]{1,0:T(8,128)(2,1)}, bf16[512,768]{1,0:T(8,128)(2,1)S(1)}, u32[]{:S(2)}, u32[]{:S(2)}) collective-permute-start(bf16[512,768]{1,0:T(8,128)(2,1)} %refs_3_.3), channel_id=1, source_target_pairs={{0,1},{1,0},{2,3},{3,2},{4,5},{5,4},{6,7},{7,6},{8,9},{9,8},{10,11... | collective-permute-start | bytes 2359304 | tf_op jit(solution)/shard_map/ppermute | solution.py:828
  23.4 20.7 %all-to-all-start = ((bf16[16,16,128]{2,1,0:T(8,128)(2,1)}), bf16[16,16,128]{2,1,0:T(8,128)(2,1)S(1)}, u32[]{:S(2)}, u32[]{:S(2)}) async-start(bf16[16,16,128]{2,1,0:T(8,128)(2,1)} %get-tuple-element.74), calls=%async_computation | async-start | bytes 131072 | tf_op jit(solution)/shard_map/all_to_all | solution.py:837
  42.7 19.4 %collective-permute-start.2 = (bf16[768,384]{1,0:T(8,128)(2,1)}, bf16[768,384]{1,0:T(8,128)(2,1)S(1)}, u32[]{:S(2)}, u32[]{:S(2)}) collective-permute-start(bf16[768,384]{1,0:T(8,128)(2,1)} %shard_map.198), channel_id=1, source_target_pairs={{0,1},{1,0},{2,3},{3,2},{4,5},{5,4},{6,7},{7,6},{8,9},{9,8},{10,11... | collective-permute-start | bytes 1769480 | tf_op jit(solution)/shard_map/ppermute | solution.py:828
  62.9 71.0 %all-to-all-start.1 = ((bf16[16,128,768]{2,1,0:T(8,128)(2,1)}), bf16[16,128,768]{2,1,0:T(8,128)(2,1)S(1)}, u32[]{:S(2)}, u32[]{:S(2)}) async-start(bf16[16,128,768]{2,1,0:T(8,128)(2,1)} %shard_map.204), calls=%async_computation.1 | async-start | bytes 6291456 | tf_op jit(solution)/shard_map/all_to_all | solution.py:837
  71.3 28.7 %collective-permute-start.3 = (bf16[768,768]{1,0:T(8,128)(2,1)}, bf16[768,768]{1,0:T(8,128)(2,1)}, u32[]{:S(2)}, u32[]{:S(2)}) collective-permute-start(bf16[768,768]{1,0:T(8,128)(2,1)} %shard_map.199), channel_id=1, source_target_pairs={{0,1},{1,0},{2,3},{3,2},{4,5},{5,4},{6,7},{7,6},{8,9},{9,8},{10,11... | collective-permute-start | bytes 3538952 | tf_op jit(solution)/shard_map/ppermute | solution.py:828
  100.0 19.5 %collective-permute-start.4 = (bf16[1024,384]{1,0:T(8,128)(2,1)}, bf16[1024,384]{1,0:T(8,128)(2,1)}, u32[]{:S(2)}, u32[]{:S(2)}) collective-permute-start(bf16[1024,384]{1,0:T(8,128)(2,1)} %shard_map.200), channel_id=1, source_target_pairs={{0,1},{1,0},{2,3},{3,2},{4,5},{5,4},{6,7},{7,6},{8,9},{9,8},{10,11... | collective-permute-start | bytes 2359304 | tf_op jit(solution)/shard_map/ppermute | solution.py:828
  119.5 14.4 %collective-permute-start.6 = (bf16[768,384]{1,0:T(8,128)(2,1)}, bf16[768,384]{1,0:T(8,128)(2,1)}, u32[]{:S(2)}, u32[]{:S(2)}) collective-permute-start(bf16[768,384]{1,0:T(8,128)(2,1)} %shard_map.205), channel_id=1, source_target_pairs={{0,1},{1,0},{2,3},{3,2},{4,5},{5,4},{6,7},{7,6},{8,9},{9,8},{10,11... | collective-permute-start | bytes 1769480 | tf_op jit(solution)/shard_map/ppermute | solution.py:828
  135.5 42.3 %all-to-all-start.2 = ((bf16[16,64,768]{2,1,0:T(8,128)(2,1)}), bf16[16,64,768]{2,1,0:T(8,128)(2,1)S(1)}, u32[]{:S(2)}, u32[]{:S(2)}) async-start(bf16[16,64,768]{2,1,0:T(8,128)(2,1)} %shard_map.206), calls=%async_computation.2 | async-start | bytes 3145728 | tf_op jit(solution)/shard_map/all_to_all | solution.py:837
  145.9 64.0 %collective-permute-start.7 = (bf16[1536,768]{1,0:T(8,128)(2,1)}, bf16[1536,768]{1,0:T(8,128)(2,1)}, u32[]{:S(2)}, u32[]{:S(2)}) collective-permute-start(bf16[1536,768]{1,0:T(8,128)(2,1)} %shard_map.209), channel_id=1, source_target_pairs={{0,1},{1,0},{2,3},{3,2},{4,5},{5,4},{6,7},{7,6},{8,9},{9,8},{10,11... | collective-permute-start | bytes 7077896 | tf_op jit(solution)/shard_map/ppermute | solution.py:828
  179.0 58.3 %all-to-all-start.3 = ((bf16[16,64,768]{2,1,0:T(8,128)(2,1)}), bf16[16,64,768]{2,1,0:T(8,128)(2,1)S(1)}, u32[]{:S(2)}, u32[]{:S(2)}) async-start(bf16[16,64,768]{2,1,0:T(8,128)(2,1)} %shard_map.208), calls=%async_computation.3 | async-start | bytes 3145728 | tf_op jit(solution)/shard_map/all_to_all | solution.py:837
  237.3 41.5 %all-to-all-start.5 = ((bf16[16,64,768]{2,1,0:T(8,128)(2,1)}), bf16[16,64,768]{2,1,0:T(8,128)(2,1)}, u32[]{:S(2)}, u32[]{:S(2)}) async-start(bf16[16,64,768]{2,1,0:T(8,128)(2,1)} %get-tuple-element.102), calls=%async_computation.5 | async-start | bytes 3145728 | tf_op jit(solution)/shard_map/all_to_all | solution.py:837
  278.8 43.3 %all-to-all-start.6 = ((bf16[16,64,768]{2,1,0:T(8,128)(2,1)}), bf16[16,64,768]{2,1,0:T(8,128)(2,1)}, u32[]{:S(2)}, u32[]{:S(2)}) async-start(bf16[16,64,768]{2,1,0:T(8,128)(2,1)} %get-tuple-element.103), calls=%async_computation.6 | async-start | bytes 3145728 | tf_op jit(solution)/shard_map/all_to_all | solution.py:837
  291.1 28.4 %collective-permute-start.8 = (bf16[384,1536]{1,0:T(8,128)(2,1)S(1)}, bf16[384,1536]{1,0:T(8,128)(2,1)S(1)}, u32[]{:S(2)}, u32[]{:S(2)}) collective-permute-start(bf16[384,1536]{1,0:T(8,128)(2,1)S(1)} %fusion.19), channel_id=1, source_target_pairs={{0,1},{1,0},{2,3},{3,2},{4,5},{5,4},{6,7},{7,6},{8,9},{9,8},{10,11... | collective-permute-start | bytes 3538952 | tf_op jit(solution)/shard_map/ppermute | solution.py:828
  320.6 29.1 %collective-permute-start.10 = (bf16[384,1536]{1,0:T(8,128)(2,1)}, bf16[384,1536]{1,0:T(8,128)(2,1)S(1)}, u32[]{:S(2)}, u32[]{:S(2)}) collective-permute-start(bf16[384,1536]{1,0:T(8,128)(2,1)} %shard_map.217), channel_id=1, source_target_pairs={{0,1},{1,0},{2,3},{3,2},{4,5},{5,4},{6,7},{7,6},{8,9},{9,8},{10,11... | collective-permute-start | bytes 3538952 | tf_op jit(solution)/shard_map/ppermute | solution.py:828
  322.1 87.3 %all-to-all-start.4 = ((bf16[16,128,768]{2,1,0:T(8,128)(2,1)}), bf16[16,128,768]{2,1,0:T(8,128)(2,1)}, u32[]{:S(2)}, u32[]{:S(2)}) async-start(bf16[16,128,768]{2,1,0:T(8,128)(2,1)} %shard_map.215), calls=%async_computation.4 | async-start | bytes 6291456 | tf_op jit(solution)/shard_map/all_to_all | solution.py:837
  337.4 27.9 %collective-permute-start.9 = (bf16[512,768]{1,0:T(8,128)(2,1)S(1)}, bf16[512,768]{1,0:T(8,128)(2,1)S(1)}, u32[]{:S(2)}, u32[]{:S(2)}) collective-permute-start(bf16[512,768]{1,0:T(8,128)(2,1)S(1)} %bitcast.77), channel_id=1, source_target_pairs={{0,1},{1,0},{2,3},{3,2},{4,5},{5,4},{6,7},{7,6},{8,9},{9,8},{10,11... | collective-permute-start | bytes 2359304 | tf_op jit(solution)/shard_map/ppermute | solution.py:828
  382.7 26.7 %collective-permute-start.12 = (bf16[768,768]{1,0:T(8,128)(2,1)}, bf16[768,768]{1,0:T(8,128)(2,1)S(1)}, u32[]{:S(2)}, u32[]{:S(2)}) collective-permute-start(bf16[768,768]{1,0:T(8,128)(2,1)} %shard_map.222), channel_id=1, source_target_pairs={{0,1},{1,0},{2,3},{3,2},{4,5},{5,4},{6,7},{7,6},{8,9},{9,8},{10,11... | collective-permute-start | bytes 3538952 | tf_op jit(solution)/shard_map/ppermute | solution.py:828
  429.7 20.2 %collective-permute-start.14 = (bf16[512,768]{1,0:T(8,128)(2,1)}, bf16[512,768]{1,0:T(8,128)(2,1)S(1)}, u32[]{:S(2)}, u32[]{:S(2)}) collective-permute-start(bf16[512,768]{1,0:T(8,128)(2,1)} %bitcast.67), channel_id=1, source_target_pairs={{0,1},{1,0},{2,3},{3,2},{4,5},{5,4},{6,7},{7,6},{8,9},{9,8},{10,11... | collective-permute-start | bytes 2359304 | tf_op jit(solution)/shard_map/ppermute | solution.py:828
  434.0 72.8 %all-to-all-start.7 = ((bf16[8,48,1920]{2,1,0:T(8,128)(2,1)}), bf16[8,48,1920]{2,1,0:T(8,128)(2,1)}, u32[]{:S(2)}, u32[]{:S(2)}) async-start(bf16[8,48,1920]{2,1,0:T(8,128)(2,1)} %fusion.18), calls=%async_computation.7 | async-start | bytes 2949120 | tf_op jit(solution)/shard_map/all_to_all | solution.py:1053
  450.8 44.9 %collective-permute-start.22 = (bf16[768,768]{1,0:T(8,128)(2,1)}, bf16[768,768]{1,0:T(8,128)(2,1)S(1)}, u32[]{:S(2)}, u32[]{:S(2)}) collective-permute-start(bf16[768,768]{1,0:T(8,128)(2,1)} %shard_map.229), channel_id=1, source_target_pairs={{0,1},{1,0},{2,3},{3,2},{4,5},{5,4},{6,7},{7,6},{8,9},{9,8},{10,11... | collective-permute-start | bytes 3538952 | tf_op jit(solution)/shard_map/ppermute | solution.py:828
  460.3 35.3 %collective-permute-start.15 = (bf16[512,768]{1,0:T(8,128)(2,1)}, bf16[512,768]{1,0:T(8,128)(2,1)}, u32[]{:S(2)}, u32[]{:S(2)}) collective-permute-start(bf16[512,768]{1,0:T(8,128)(2,1)} %bitcast.76), channel_id=1, source_target_pairs={{0,1},{1,0},{2,3},{3,2},{4,5},{5,4},{6,7},{7,6},{8,9},{9,8},{10,11... | collective-permute-start | bytes 2359304 | tf_op jit(solution)/shard_map/ppermute | solution.py:828
  473.4 13.8 %collective-permute-start.21 = (f32[48,768]{1,0:T(8,128)S(1)}, f32[48,768]{1,0:T(8,128)S(1)}, u32[]{:S(2)}, u32[]{:S(2)}) collective-permute-start(f32[48,768]{1,0:T(8,128)S(1)} %add_add_fusion.1), channel_id=1, source_target_pairs={{0,24},{2,26},{4,28},{6,30},{8,16},{10,18},{12,20},{14,22},{16,8},... | collective-permute-start | bytes 442376 | tf_op jit(solution)/shard_map/ppermute | solution.py:847
  (52 other events, 431.2 us)
Sparse Core Ops, SparseCore 0:
  14.0 46.4 all-gather.1

commit v2 on v1

--- a/solution.py
+++ b/solution.py
@@ -550,7 +550,7 @@
             out_ref[...] = total
 
 
-def add_call(own, pairs):
+def add_call(own, pairs, held=()):
     rows, cols = own.shape
     block = pl.BlockSpec((rows // 2, cols), lambda i: (i, 0))
     half = pl.BlockSpec(
@@ -559,14 +559,16 @@
     return pl.pallas_call(
         partial(add_kernel, len(pairs)),
         grid=(2,),
-        in_specs=[block] + [half] * (2 * len(pairs)),
+        in_specs=[block]
+        + [half] * (2 * len(pairs))
+        + [pl.BlockSpec(memory_space=pl.ANY)] * len(held),
         out_specs=block,
         out_shape=shape(own.shape, F32),
         compiler_params=pltpu.CompilerParams(
             dimension_semantics=("arbitrary",), vmem_limit_bytes=40 * 1024 * 1024
         ),
         cost_estimate=cost(0),
-    )(own, *[part for pair in pairs for part in pair])
+    )(own, *[part for pair in pairs for part in pair], *held)
 
 
 def combine_kernel(ranks, chunks, rank_ref, by_col_ref, *refs):
@@ -1070,10 +1072,10 @@
     weight_total = jnp.sum(shards.astype(F32), axis=0)
     qkv_grad = weight_total[:, : 3 * heads_wide].reshape(-1, 3, heads_wide)[:, :, :heads_true]
     out_part = jnp.split(weight_total[:, 3 * heads_wide :], ranks, axis=1)
-    attn_out_grad = out_part[0]
-    for shift in range(1, ranks):
-        attn_out_grad = attn_out_grad + sent(out_part[shift], ranks - shift)
-    attn_out_grad = attn_out_grad[:, :heads_true].T
+    out_part = out_part[:1] + [
+        sent(out_part[shift], ranks - shift) for shift in range(1, ranks)
+    ]
+    attn_out_grad = sum(out_part)[:, :heads_true].T
 
     moe_own, moe_other = combine_call(
         rank_arr, ranks, by_col, [results], own, 0, held=dnormed_pieces
@@ -1086,7 +1088,7 @@
         mixed = mixed + piece.astype(F32)
 
     in_grad = add_call(in_own_grad, list(zip(firsts, seconds)))
-    out_grad = add_call(out_own_grad, list(zip(thirds, fourths)))
+    out_grad = add_call(out_own_grad, list(zip(thirds, fourths)), out_part[1:])
     return (
         mixed.astype(BF),
         grad_tokens,

time: 527 us -> 528 us (level)
    unnamed x87 -> x89, local copies, waits for them, and re-layouts: 24.3 us -> 24.3 us
  transfers between devices with their start and end apart: 34 -> 34, of which waited for: 17 -> 18; matrix products, arithmetic and copies ran while one was open for 11% -> 11% of each run, Pallas kernels for 39% -> 38%
where the time goes in v2:
time: 528 us; the launch traced here: 522 us
  Pallas kernels  210 us (40%)
  waiting for transfers between devices  125 us (24%)
  starting transfers between devices  88.6 us (17%)
  local copies, waits for them, and re-layouts  36.8 us (7%)
  matrix products  32.9 us (6%)
  between operations  15 us (3%)
  other arithmetic  12.9 us (2%)
    pallas_call x11, Pallas kernels, whole(): pl.pallas_call(body, out_shape=outs, in_specs=[pl.BlockSpec(memory_space=...  107 us
    ppermute x17, waiting for transfers between devices, sent(): lax.ppermute(values, 'mp', [(i, (i + shift) % ranks) for i in range(ranks)])  85.5 us
    pallas_call x3, Pallas kernels, expert_call(): pl.pallas_call(partial(expert_kernel, steps, experts, chunk * slots, firs...  77.9 us
    all_to_all x7, starting transfers between devices, to_experts(): return lax.all_to_all(rows, 'dp', split_axis=0, concat_axis=0, tiled=True)  52.3 us
    dot_general x5, matrix products, rows_dot(): lax.dot_general(left, right, (((0,), (0,)), ((), ())), preferred_element_...  32.9 us
    all_to_all x7, waiting for transfers between devices, to_experts(): return lax.all_to_all(rows, 'dp', split_axis=0, concat_axis=0, tiled=True)  25.9 us
    unnamed x89, local copies, waits for them, and re-layouts  24.3 us
    ppermute x17, starting transfers between devices, sent(): lax.ppermute(values, 'mp', [(i, (i + shift) % ranks) for i in range(ranks)])  23.1 us
  transfers between devices with their start and end apart: 34, of which 18 were waited for; matrix products, arithmetic and copies ran while one was open for 11% of the time, Pallas kernels for 38%

profile of v2, /device:TPU:0, one launch (start us, length us, event | category | flops | bytes accessed | tf_op | source)
XLA Modules:
  0.0 522.0 jit_solution(15025929434680531284)
XLA Ops:
  44.1 7.4 %collective-permute-done.5.refs_3_ = bf16[512,768]{1,0:T(8,128)(2,1)S(1)} collective-permute-done((bf16[512,768]{1,0:T(8,128)(2,1)}, bf16[512,768]{1,0:T(8,128)(2,1)S(1)}, u32[]{:S(2)}, u32[]{:S(2)}) %collective-permute-start.5) | collective-permute-done | bytes 786464 | tf_op jit(solution)/shard_map/ppermute | solution.py:830
  52.4 9.3 %shard_map.203.refs_0_ = bf16[16,128,768]{2,1,0:T(8,128)(2,1)} custom-call(s32[1]{0:T(128)} %bitcast.refs_0_, f32[16,1024]{1,0:T(8,128)} %get-tuple-element.66.refs_2_.refs_1_, bf16[512,768]{1,0:T(8,128)(2,1)} %refs_3_.3, bf16[512,768]{1,0:T(8,128)(2,1)} %copy-done.37, bf16[16,16,128]{2,1,0:T(8,128)(2,1)} %copy-done.28, bf16[512,768]{1,0:T(8,128)(2,1)} %copy-done.26, ...), custom_call_target="tpu_custom_call" | custom-call | flops 9900000256 | tf_op jit(solution)/shard_map/pallas_call | solution.py:52
  72.8 16.3 %shard_map.196 = (bf16[1024,1152]{1,0:T(8,128)(2,1)}, bf16[1024,384]{1,0:T(8,128)(2,1)}, f32[8,1024]{1,0:T(8,128)}, f32[16,2048]{1,0:T(8,128)}) custom-call(s32[1]{0:T(128)} %bitcast.refs_0_, f32[1,768]{1,0:T(1,128)} %reshape.63.refs_1_, bf16[768,1920]{1,0:T(8,128)(2,1)} %all-gather.2.cloned.1.call-done.refs_2_.refs_1_, bf16[16,128]{1,0:T(8,128)(2,1)} %pad.12.refs_3_, ...), custom_call_target="tpu_custom_call" | custom-call | flops 17600000000 | tf_op jit(solution)/shard_map/pallas_call | solution.py:52
  91.3 8.7 %collective-permute-done.3.refs_1_ = bf16[768,768]{1,0:T(8,128)(2,1)} collective-permute-done((bf16[768,768]{1,0:T(8,128)(2,1)}, bf16[768,768]{1,0:T(8,128)(2,1)}, u32[]{:S(2)}, u32[]{:S(2)}) %collective-permute-start.3) | collective-permute-done | bytes 1179680 | tf_op jit(solution)/shard_map/ppermute | solution.py:830
  104.5 15.0 %collective-permute-done.4.refs_6_.refs_1_.refs_7_ = bf16[1024,384]{1,0:T(8,128)(2,1)} collective-permute-done((bf16[1024,384]{1,0:T(8,128)(2,1)}, bf16[1024,384]{1,0:T(8,128)(2,1)}, u32[]{:S(2)}, u32[]{:S(2)}) %collective-permute-start.4) | collective-permute-done | bytes 786464 | tf_op jit(solution)/shard_map/ppermute | solution.py:830
  121.0 12.3 %shard_map.201 = (f32[512,768]{1,0:T(8,128)}, bf16[16,64,768]{2,1,0:T(8,128)(2,1)}, bf16[16,64,768]{2,1,0:T(8,128)(2,1)}) custom-call(s32[1]{0:T(128)} %bitcast.refs_0_, f32[1,768]{1,0:T(1,128)} %reshape.61.refs_1_, f32[16,1024]{1,0:T(8,128)} %get-tuple-element.66.refs_2_.refs_1_, bf16[512,768]{1,0:T(8,128)(2,1)} %refs_2_.3, bf16[512,768]{1,0:T(8,128)(2,1)} %copy-done.26, ...), custom_call_target="tpu_custom_call" | custom-call | flops 13200000000 | tf_op jit(solution)/shard_map/pallas_call | solution.py:52
  135.5 10.3 %all-to-all-start.2 = ((bf16[16,64,768]{2,1,0:T(8,128)(2,1)}), bf16[16,64,768]{2,1,0:T(8,128)(2,1)S(1)}, u32[]{:S(2)}, u32[]{:S(2)}) async-start(bf16[16,64,768]{2,1,0:T(8,128)(2,1)} %shard_map.206), calls=%async_computation.2 | async-start | bytes 3145728 | tf_op jit(solution)/shard_map/all_to_all | solution.py:839
  151.9 25.9 %all-to-all-done.2.refs_1_.rows_ref = bf16[16,64,768]{2,1,0:T(8,128)(2,1)S(1)} async-done(((bf16[16,64,768]{2,1,0:T(8,128)(2,1)}), bf16[16,64,768]{2,1,0:T(8,128)(2,1)S(1)}, u32[]{:S(2)}, u32[]{:S(2)}) %all-to-all-start.2) | async-done | bytes 1572896 | tf_op jit(solution)/shard_map/all_to_all | solution.py:839
  179.0 9.5 %all-to-all-start.3 = ((bf16[16,64,768]{2,1,0:T(8,128)(2,1)}), bf16[16,64,768]{2,1,0:T(8,128)(2,1)S(1)}, u32[]{:S(2)}, u32[]{:S(2)}) async-start(bf16[16,64,768]{2,1,0:T(8,128)(2,1)} %shard_map.208), calls=%async_computation.3 | async-start | bytes 3145728 | tf_op jit(solution)/shard_map/all_to_all | solution.py:839
  189.4 20.4 %shard_map.210 = (bf16[2048,768]{1,0:T(8,128)(2,1)}, bf16[2048,768]{1,0:T(8,128)(2,1)}, bf16[2,2048,1536]{2,1,0:T(8,128)(2,1)}, bf16[2,2048,1536]{2,1,0:T(8,128)...) custom-call(s32[1]{0:T(128)} %bitcast.6.ids_ref, bf16[16,64,768]{2,1,0:T(8,128)(2,1)} %copy-done.13, ...), custom_call_target="tpu_custom_call" | custom-call | flops 4400000000 | tf_op jit(solution)/shard_map/pallas_call | solution.py:456
  214.4 22.8 %shard_map.213 = (bf16[2,2048,1536]{2,1,0:T(8,128)(2,1)}, bf16[2,2048,1536]{2,1,0:T(8,128)(2,1)}, bf16[16,64,768]{2,1,0:T(8,128)(2,1)}, f32[16,768]{1,0:T(8,128)}, bf16[16,128,768]{2,1,0:T(8,128)(2,1)}) custom-call(s32[1]{0:T(128)} %bitcast.6.ids_ref, bf16[16,64,768]{2,1,0:T(8,128)(2,1)} %copy-done.13, ...), custom_call_target="tpu_custom_call", output_to_operand_aliasing={{0}: (12, {}), {1}: (13, {})} | custom-call | flops 4400000000 | tf_op jit(solution)/shard_map/pallas_call | solution.py:456
  237.2 6.7 %all-to-all-start.5 = ((bf16[16,64,768]{2,1,0:T(8,128)(2,1)}), bf16[16,64,768]{2,1,0:T(8,128)(2,1)}, u32[]{:S(2)}, u32[]{:S(2)}) async-start(bf16[16,64,768]{2,1,0:T(8,128)(2,1)} %get-tuple-element.102), calls=%async_computation.5 | async-start | bytes 3145728 | tf_op jit(solution)/shard_map/all_to_all | solution.py:839
  243.9 34.6 %shard_map.214 = (bf16[2048,768]{1,0:T(8,128)(2,1)}, bf16[2048,768]{1,0:T(8,128)(2,1)}, bf16[2,2048,1536]{2,1,0:T(8,128)(2,1)}, bf16[2,2048,1536]{2,1,0:T(8,128)...) custom-call(s32[1]{0:T(128)} %bitcast.6.ids_ref, ...), custom_call_target="tpu_custom_call", output_to_operand_aliasing={{0}: (9, {}), {1}: (10, {}), {2}: (11, {}), {3}: (12, {}), ... | custom-call | flops 38499999744 | tf_op jit(solution)/shard_map/pallas_call | solution.py:456
  278.6 6.8 %all-to-all-start.6 = ((bf16[16,64,768]{2,1,0:T(8,128)(2,1)}), bf16[16,64,768]{2,1,0:T(8,128)(2,1)}, u32[]{:S(2)}, u32[]{:S(2)}) async-start(bf16[16,64,768]{2,1,0:T(8,128)(2,1)} %get-tuple-element.103), calls=%async_computation.6 | async-start | bytes 3145728 | tf_op jit(solution)/shard_map/all_to_all | solution.py:839
  305.4 14.0 %collective-permute-done.8.refs_1_.refs_4_.refs_0_ = bf16[384,1536]{1,0:T(8,128)(2,1)S(1)} collective-permute-done((bf16[384,1536]{1,0:T(8,128)(2,1)S(1)}, bf16[384,1536]{1,0:T(8,128)(2,1)S(1)}, u32[]{:S(2)}, u32[]{:S(2)}) %collective-permute-start.8) | collective-permute-done | bytes 1179680 | tf_op jit(solution)/shard_map/ppermute | solution.py:830
  328.0 8.1 %shard_map.216 = (f32[512,768]{1,0:T(8,128)}, bf16[1,512,768]{2,1,0:T(8,128)(2,1)}) custom-call(s32[1]{0:T(128)} %bitcast.refs_0_, f32[1024,128]{1,0:T(8,128)} %get-tuple-element.71.refs_1_, bf16[16,64,768]{2,1,0:T(8,128)(2,1)} %all-to-all-done.5.refs_2_, bf16[16,64,768]{2,1,0:T(8,128)(2,1)} %all-to-all-done.6.refs_3_, bf16[384,1536]{1,0:T(8,128)(2,1)} %copy-done.2, ...), custom_call_target="tpu_custom_call" | custom-call | flops 8800000000 | tf_op jit(solution)/shard_map/pallas_call | solution.py:52
  337.8 9.6 %fusion.2.refs_7_.own_ref = f32[768,1536]{1,0:T(8,128)} fusion(bf16[2048,768]{1,0:T(8,128)(2,1)} %shard_map.219, bf16[2,2048,1536]{2,1,0:T(8,128)(2,1)} %get-tuple-element.98), kind=kOutput, calls=%fused_computation.2 | convolution fusion | flops 4831838208 | bytes 14155776 | tf_op jit(solution)/shard_map/dot_general | solution.py:961
  349.6 15.6 %collective-permute-done.9.refs_5_ = bf16[512,768]{1,0:T(8,128)(2,1)S(1)} collective-permute-done((bf16[512,768]{1,0:T(8,128)(2,1)S(1)}, bf16[512,768]{1,0:T(8,128)(2,1)S(1)}, u32[]{:S(2)}, u32[]{:S(2)}) %collective-permute-start.9) | collective-permute-done | bytes 786464 | tf_op jit(solution)/shard_map/ppermute | solution.py:830
  373.1 8.7 %fusion.refs_8_.own_ref = f32[1536,768]{1,0:T(8,128)} fusion(bf16[2048,768]{1,0:T(8,128)(2,1)S(1)} %copy-done.15, bf16[2,2048,1536]{2,1,0:T(8,128)(2,1)} %get-tuple-element.104), kind=kOutput, calls=%fused_computation | convolution fusion | flops 4831838208 | bytes 14155776 | tf_op jit(solution)/shard_map/dot_general | solution.py:961
  384.0 21.2 %shard_map.221 = (bf16[1024,1152]{1,0:T(8,128)(2,1)}, f32[16,128]{1,0:T(8,128)}) custom-call(s32[1]{0:T(128)} %bitcast.refs_0_, bf16[1024,1152]{1,0:T(8,128)(2,1)} %get-tuple-element.99.refs_1_, f32[8,1024]{1,0:T(8,128)} %get-tuple-element.100.refs_2_, f32[16,2048]{1,0:T(8,128)} %get-tuple-element.101.refs_3_, s32[1,2048]{1,0:T(1,128)} %bitcast.75, ...), custom_call_target="tpu_custom_call" | custom-call | flops 22000001024 | tf_op jit(solution)/shard_map/pallas_call | solution.py:52
  410.4 8.1 %shard_map.223.refs_6_ = bf16[768,1920]{1,0:T(8,128)(2,1)} custom-call(s32[1]{0:T(128)} %bitcast.refs_0_, f32[1,768]{1,0:T(1,128)} %reshape.63.refs_1_, bf16[1024,1152]{1,0:T(8,128)(2,1)} %get-tuple-element.110.refs_2_, bf16[512,768]{1,0:T(8,128)(2,1)} %get-tuple-element.112.refs_3_, bf16[512,768]{1,0:T(8,128)(2,1)} %refs_2_.3, bf16[512,768]{1,0:T(8,128)(2,1)} %copy-done.26, ...), custom_call_target="tpu_custom_call" | custom-call | flops 8800000000 | tf_op jit(solution)/shard_map/pallas_call | solution.py:52
  421.1 7.3 %shard_map.224 = (f32[512,768]{1,0:T(8,128)}, bf16[1,512,768]{2,1,0:T(8,128)(2,1)}, f32[24,768]{1,0:T(8,128)}) custom-call(s32[1]{0:T(128)} %bitcast.refs_0_, bf16[768,1920]{1,0:T(8,128)(2,1)} %all-gather.2.cloned.1.call-done.refs_2_.refs_1_, bf16[1024,1152]{1,0:T(8,128)(2,1)} %get-tuple-element.110.refs_2_, f32[16,128]{1,0:T(8,128)} %get-tuple-element.111.refs_3_, ...), custom_call_target="tpu_custom_call" | custom-call | flops 7699999744 | tf_op jit(solution)/shard_map/pallas_call | solution.py:52
  439.0 10.7 %collective-permute-done.14.refs_3_.refs_5_.refs_1_ = bf16[512,768]{1,0:T(8,128)(2,1)S(1)} collective-permute-done((bf16[512,768]{1,0:T(8,128)(2,1)}, bf16[512,768]{1,0:T(8,128)(2,1)S(1)}, u32[]{:S(2)}, u32[]{:S(2)}) %collective-permute-start.14) | collective-permute-done | bytes 786464 | tf_op jit(solution)/shard_map/ppermute | solution.py:830
  451.6 8.6 %shard_map.226 = (f32[512,768]{1,0:T(8,128)}, bf16[1,512,768]{2,1,0:T(8,128)(2,1)}) custom-call(s32[1]{0:T(128)} %bitcast.refs_0_, f32[1024,128]{1,0:T(8,128)} %get-tuple-element.71.refs_1_, bf16[16,128,768]{2,1,0:T(8,128)(2,1)} %all-to-all-done.4.refs_8_.refs_2_, bf16[512,768]{1,0:T(8,128)(2,1)} %copy-done.17), custom_call_target="tpu_custom_call" | custom-call | tf_op jit(solution)/shard_map/pallas_call | solution.py:52
  (204 shorter events, 188.9 us)
Async XLA Ops:
  7.2 54.9 %all-gather.2.cloned.1.call-start = ((), (), s32[]{:S(2)}) async-start(), calls=%async_computation.8 | async-start | bytes 3133440 | tf_op jit(solution)/shard_map/all_gather | solution.py:866
  13.9 27.9 %collective-permute-start = (bf16[512,768]{1,0:T(8,128)(2,1)}, bf16[512,768]{1,0:T(8,128)(2,1)S(1)}, u32[]{:S(2)}, u32[]{:S(2)}) collective-permute-start(bf16[512,768]{1,0:T(8,128)(2,1)} %refs_2_.3), channel_id=1, source_target_pairs={{0,1},{1,0},{2,3},{3,2},{4,5},{5,4},{6,7},{7,6},{8,9},{9,8},{10,11... | collective-permute-start | bytes 2359304 | tf_op jit(solution)/shard_map/ppermute | solution.py:830
  16.0 35.5 %collective-permute-start.5 = (bf16[512,768]{1,0:T(8,128)(2,1)}, bf16[512,768]{1,0:T(8,128)(2,1)S(1)}, u32[]{:S(2)}, u32[]{:S(2)}) collective-permute-start(bf16[512,768]{1,0:T(8,128)(2,1)} %refs_3_.3), channel_id=1, source_target_pairs={{0,1},{1,0},{2,3},{3,2},{4,5},{5,4},{6,7},{7,6},{8,9},{9,8},{10,11... | collective-permute-start | bytes 2359304 | tf_op jit(solution)/shard_map/ppermute | solution.py:830
  23.4 20.7 %all-to-all-start = ((bf16[16,16,128]{2,1,0:T(8,128)(2,1)}), bf16[16,16,128]{2,1,0:T(8,128)(2,1)S(1)}, u32[]{:S(2)}, u32[]{:S(2)}) async-start(bf16[16,16,128]{2,1,0:T(8,128)(2,1)} %get-tuple-element.74), calls=%async_computation | async-start | bytes 131072 | tf_op jit(solution)/shard_map/all_to_all | solution.py:839
  42.7 19.4 %collective-permute-start.2 = (bf16[768,384]{1,0:T(8,128)(2,1)}, bf16[768,384]{1,0:T(8,128)(2,1)S(1)}, u32[]{:S(2)}, u32[]{:S(2)}) collective-permute-start(bf16[768,384]{1,0:T(8,128)(2,1)} %shard_map.198), channel_id=1, source_target_pairs={{0,1},{1,0},{2,3},{3,2},{4,5},{5,4},{6,7},{7,6},{8,9},{9,8},{10,11... | collective-permute-start | bytes 1769480 | tf_op jit(solution)/shard_map/ppermute | solution.py:830
  62.9 71.0 %all-to-all-start.1 = ((bf16[16,128,768]{2,1,0:T(8,128)(2,1)}), bf16[16,128,768]{2,1,0:T(8,128)(2,1)S(1)}, u32[]{:S(2)}, u32[]{:S(2)}) async-start(bf16[16,128,768]{2,1,0:T(8,128)(2,1)} %shard_map.204), calls=%async_computation.1 | async-start | bytes 6291456 | tf_op jit(solution)/shard_map/all_to_all | solution.py:839
  71.3 28.7 %collective-permute-start.3 = (bf16[768,768]{1,0:T(8,128)(2,1)}, bf16[768,768]{1,0:T(8,128)(2,1)}, u32[]{:S(2)}, u32[]{:S(2)}) collective-permute-start(bf16[768,768]{1,0:T(8,128)(2,1)} %shard_map.199), channel_id=1, source_target_pairs={{0,1},{1,0},{2,3},{3,2},{4,5},{5,4},{6,7},{7,6},{8,9},{9,8},{10,11... | collective-permute-start | bytes 3538952 | tf_op jit(solution)/shard_map/ppermute | solution.py:830
  100.0 19.5 %collective-permute-start.4 = (bf16[1024,384]{1,0:T(8,128)(2,1)}, bf16[1024,384]{1,0:T(8,128)(2,1)}, u32[]{:S(2)}, u32[]{:S(2)}) collective-permute-start(bf16[1024,384]{1,0:T(8,128)(2,1)} %shard_map.200), channel_id=1, source_target_pairs={{0,1},{1,0},{2,3},{3,2},{4,5},{5,4},{6,7},{7,6},{8,9},{9,8},{10,11... | collective-permute-start | bytes 2359304 | tf_op jit(solution)/shard_map/ppermute | solution.py:830
  119.5 14.4 %collective-permute-start.6 = (bf16[768,384]{1,0:T(8,128)(2,1)}, bf16[768,384]{1,0:T(8,128)(2,1)}, u32[]{:S(2)}, u32[]{:S(2)}) collective-permute-start(bf16[768,384]{1,0:T(8,128)(2,1)} %shard_map.205), channel_id=1, source_target_pairs={{0,1},{1,0},{2,3},{3,2},{4,5},{5,4},{6,7},{7,6},{8,9},{9,8},{10,11... | collective-permute-start | bytes 1769480 | tf_op jit(solution)/shard_map/ppermute | solution.py:830
  135.5 42.3 %all-to-all-start.2 = ((bf16[16,64,768]{2,1,0:T(8,128)(2,1)}), bf16[16,64,768]{2,1,0:T(8,128)(2,1)S(1)}, u32[]{:S(2)}, u32[]{:S(2)}) async-start(bf16[16,64,768]{2,1,0:T(8,128)(2,1)} %shard_map.206), calls=%async_computation.2 | async-start | bytes 3145728 | tf_op jit(solution)/shard_map/all_to_all | solution.py:839
  145.9 64.0 %collective-permute-start.7 = (bf16[1536,768]{1,0:T(8,128)(2,1)}, bf16[1536,768]{1,0:T(8,128)(2,1)}, u32[]{:S(2)}, u32[]{:S(2)}) collective-permute-start(bf16[1536,768]{1,0:T(8,128)(2,1)} %shard_map.209), channel_id=1, source_target_pairs={{0,1},{1,0},{2,3},{3,2},{4,5},{5,4},{6,7},{7,6},{8,9},{9,8},{10,11... | collective-permute-start | bytes 7077896 | tf_op jit(solution)/shard_map/ppermute | solution.py:830
  179.0 58.2 %all-to-all-start.3 = ((bf16[16,64,768]{2,1,0:T(8,128)(2,1)}), bf16[16,64,768]{2,1,0:T(8,128)(2,1)S(1)}, u32[]{:S(2)}, u32[]{:S(2)}) async-start(bf16[16,64,768]{2,1,0:T(8,128)(2,1)} %shard_map.208), calls=%async_computation.3 | async-start | bytes 3145728 | tf_op jit(solution)/shard_map/all_to_all | solution.py:839
  237.2 41.4 %all-to-all-start.5 = ((bf16[16,64,768]{2,1,0:T(8,128)(2,1)}), bf16[16,64,768]{2,1,0:T(8,128)(2,1)}, u32[]{:S(2)}, u32[]{:S(2)}) async-start(bf16[16,64,768]{2,1,0:T(8,128)(2,1)} %get-tuple-element.102), calls=%async_computation.5 | async-start | bytes 3145728 | tf_op jit(solution)/shard_map/all_to_all | solution.py:839
  278.6 43.4 %all-to-all-start.6 = ((bf16[16,64,768]{2,1,0:T(8,128)(2,1)}), bf16[16,64,768]{2,1,0:T(8,128)(2,1)}, u32[]{:S(2)}, u32[]{:S(2)}) async-start(bf16[16,64,768]{2,1,0:T(8,128)(2,1)} %get-tuple-element.103), calls=%async_computation.6 | async-start | bytes 3145728 | tf_op jit(solution)/shard_map/all_to_all | solution.py:839
  291.0 28.4 %collective-permute-start.8 = (bf16[384,1536]{1,0:T(8,128)(2,1)S(1)}, bf16[384,1536]{1,0:T(8,128)(2,1)S(1)}, u32[]{:S(2)}, u32[]{:S(2)}) collective-permute-start(bf16[384,1536]{1,0:T(8,128)(2,1)S(1)} %fusion.19), channel_id=1, source_target_pairs={{0,1},{1,0},{2,3},{3,2},{4,5},{5,4},{6,7},{7,6},{8,9},{9,8},{10,11... | collective-permute-start | bytes 3538952 | tf_op jit(solution)/shard_map/ppermute | solution.py:830
  320.5 29.1 %collective-permute-start.10 = (bf16[384,1536]{1,0:T(8,128)(2,1)}, bf16[384,1536]{1,0:T(8,128)(2,1)S(1)}, u32[]{:S(2)}, u32[]{:S(2)}) collective-permute-start(bf16[384,1536]{1,0:T(8,128)(2,1)} %shard_map.217), channel_id=1, source_target_pairs={{0,1},{1,0},{2,3},{3,2},{4,5},{5,4},{6,7},{7,6},{8,9},{9,8},{10,11... | collective-permute-start | bytes 3538952 | tf_op jit(solution)/shard_map/ppermute | solution.py:830
  322.0 87.3 %all-to-all-start.4 = ((bf16[16,128,768]{2,1,0:T(8,128)(2,1)}), bf16[16,128,768]{2,1,0:T(8,128)(2,1)}, u32[]{:S(2)}, u32[]{:S(2)}) async-start(bf16[16,128,768]{2,1,0:T(8,128)(2,1)} %shard_map.215), calls=%async_computation.4 | async-start | bytes 6291456 | tf_op jit(solution)/shard_map/all_to_all | solution.py:839
  337.3 27.9 %collective-permute-start.9 = (bf16[512,768]{1,0:T(8,128)(2,1)S(1)}, bf16[512,768]{1,0:T(8,128)(2,1)S(1)}, u32[]{:S(2)}, u32[]{:S(2)}) collective-permute-start(bf16[512,768]{1,0:T(8,128)(2,1)S(1)} %bitcast.77), channel_id=1, source_target_pairs={{0,1},{1,0},{2,3},{3,2},{4,5},{5,4},{6,7},{7,6},{8,9},{9,8},{10,11... | collective-permute-start | bytes 2359304 | tf_op jit(solution)/shard_map/ppermute | solution.py:830
  382.5 26.7 %collective-permute-start.12 = (bf16[768,768]{1,0:T(8,128)(2,1)}, bf16[768,768]{1,0:T(8,128)(2,1)S(1)}, u32[]{:S(2)}, u32[]{:S(2)}) collective-permute-start(bf16[768,768]{1,0:T(8,128)(2,1)} %shard_map.222), channel_id=1, source_target_pairs={{0,1},{1,0},{2,3},{3,2},{4,5},{5,4},{6,7},{7,6},{8,9},{9,8},{10,11... | collective-permute-start | bytes 3538952 | tf_op jit(solution)/shard_map/ppermute | solution.py:830
  429.5 20.2 %collective-permute-start.14 = (bf16[512,768]{1,0:T(8,128)(2,1)}, bf16[512,768]{1,0:T(8,128)(2,1)S(1)}, u32[]{:S(2)}, u32[]{:S(2)}) collective-permute-start(bf16[512,768]{1,0:T(8,128)(2,1)} %bitcast.67), channel_id=1, source_target_pairs={{0,1},{1,0},{2,3},{3,2},{4,5},{5,4},{6,7},{7,6},{8,9},{9,8},{10,11... | collective-permute-start | bytes 2359304 | tf_op jit(solution)/shard_map/ppermute | solution.py:830
  433.8 69.3 %all-to-all-start.7 = ((bf16[8,48,1920]{2,1,0:T(8,128)(2,1)}), bf16[8,48,1920]{2,1,0:T(8,128)(2,1)}, u32[]{:S(2)}, u32[]{:S(2)}) async-start(bf16[8,48,1920]{2,1,0:T(8,128)(2,1)} %fusion.18), calls=%async_computation.7 | async-start | bytes 2949120 | tf_op jit(solution)/shard_map/all_to_all | solution.py:1055
  450.6 44.9 %collective-permute-start.22 = (bf16[768,768]{1,0:T(8,128)(2,1)}, bf16[768,768]{1,0:T(8,128)(2,1)S(1)}, u32[]{:S(2)}, u32[]{:S(2)}) collective-permute-start(bf16[768,768]{1,0:T(8,128)(2,1)} %shard_map.229), channel_id=1, source_target_pairs={{0,1},{1,0},{2,3},{3,2},{4,5},{5,4},{6,7},{7,6},{8,9},{9,8},{10,11... | collective-permute-start | bytes 3538952 | tf_op jit(solution)/shard_map/ppermute | solution.py:830
  460.2 35.3 %collective-permute-start.15 = (bf16[512,768]{1,0:T(8,128)(2,1)}, bf16[512,768]{1,0:T(8,128)(2,1)}, u32[]{:S(2)}, u32[]{:S(2)}) collective-permute-start(bf16[512,768]{1,0:T(8,128)(2,1)} %bitcast.76), channel_id=1, source_target_pairs={{0,1},{1,0},{2,3},{3,2},{4,5},{5,4},{6,7},{7,6},{8,9},{9,8},{10,11... | collective-permute-start | bytes 2359304 | tf_op jit(solution)/shard_map/ppermute | solution.py:830
  473.2 13.9 %collective-permute-start.21 = (f32[48,768]{1,0:T(8,128)S(1)}, f32[48,768]{1,0:T(8,128)S(1)}, u32[]{:S(2)}, u32[]{:S(2)}) collective-permute-start(f32[48,768]{1,0:T(8,128)S(1)} %add_add_fusion.1), channel_id=1, source_target_pairs={{0,24},{2,26},{4,28},{6,30},{8,16},{10,18},{12,20},{14,22},{16,8},... | collective-permute-start | bytes 442376 | tf_op jit(solution)/shard_map/ppermute | solution.py:849
  (53 other events, 439.3 us)
Sparse Core Ops, SparseCore 0:
  14.0 46.4 all-gather.1

commit v3 on v1

--- a/solution.py
+++ b/solution.py
@@ -538,35 +538,48 @@
     )(*parts, *earlier)
 
 
-def add_kernel(pairs, own_ref, *refs):
+def add_kernel(places, own_ref, *refs):
     out_ref = refs[-1]
+    half = own_ref.shape[0]
     for index in range(2):
 
         @pl.when(pl.program_id(0) == index)
         def _():
-            total = own_ref[...]
-            for pair in range(pairs):
-                total = total + refs[2 * pair + index][...].astype(F32)
-            out_ref[...] = total
-
-
-def add_call(own, pairs):
+            out_ref[...] = own_ref[...]
+            for (first, last), ref in zip(places, refs):
+                start, stop = max(first, index * half), min(last, (index + 1) * half)
+                if start < stop:
+                    out_ref[start - index * half : stop - index * half, :] += ref[
+                        start - first : stop - first, :
+                    ].astype(F32)
+
+
+def add_call(own, groups):
     rows, cols = own.shape
-    block = pl.BlockSpec((rows // 2, cols), lambda i: (i, 0))
-    half = pl.BlockSpec(
-        (rows // 2, cols), lambda i: (0, 0), pipeline_mode=pl.Buffered(1)
-    )
+    half = rows // 2
+    places, parts = [], []
+    for group in groups:
+        start = 0
+        for part in group:
+            places.append((start, start + part.shape[0]))
+            parts.append(part)
+            start += part.shape[0]
+    block = pl.BlockSpec((half, cols), lambda i: (i, 0))
     return pl.pallas_call(
-        partial(add_kernel, len(pairs)),
+        partial(add_kernel, places),
         grid=(2,),
-        in_specs=[block] + [half] * (2 * len(pairs)),
+        in_specs=[block]
+        + [
+            pl.BlockSpec(part.shape, lambda i: (0, 0), pipeline_mode=pl.Buffered(1))
+            for part in parts
+        ],
         out_specs=block,
         out_shape=shape(own.shape, F32),
         compiler_params=pltpu.CompilerParams(
             dimension_semantics=("arbitrary",), vmem_limit_bytes=40 * 1024 * 1024
         ),
         cost_estimate=cost(0),
-    )(own, *[part for pair in pairs for part in pair])
+    )(own, *parts)
 
 
 def combine_kernel(ranks, chunks, rank_ref, by_col_ref, *refs):
@@ -792,6 +805,17 @@
     small_ref[8:24, 0:LANES] = table_ref[...]
 
 
+def back_and_grad_kernel(ranks, head_count, rank_ref, qkv_ref, log_ref, offsets_ref, *refs):
+    buckets_ref, heads, refs = refs[0], refs[1 : 1 + ranks], refs[1 + ranks :]
+    gain_ref, dbranch_ref, pieces, refs = refs[0], refs[1], refs[2 : 2 + 2 * ranks], refs[2 + 2 * ranks :]
+    dqkv, table_ref, grad_ref, *scratch, normed_t = refs
+    attend_back_kernel(
+        ranks, head_count, rank_ref, qkv_ref, log_ref, offsets_ref, buckets_ref, *heads, dqkv,
+        table_ref, *scratch,
+    )
+    project_grad_kernel(ranks, rank_ref, gain_ref, dqkv, dbranch_ref, *pieces, grad_ref, normed_t)
+
+
 def token_back_kernel(ranks, rank_ref, gain_ref, tokens_ref, dmid_ref, part_ref, *refs):
     received, out_ref = refs[: ranks - 1], refs[ranks - 1]
     own = tokens_ref.shape[0]
@@ -992,15 +1016,19 @@
     )
     dheads = [dheads, *exchanged(other_dheads)]
     thirds = [
-        sent(after(grad[: hidden // 2], *dheads[1:]), ranks - 1 - j)
+        sent(after(grad[: 5 * hidden // 8], *dheads[1:]), ranks - 1 - j)
         for j, grad in enumerate(out_grads)
     ]
     early = jnp.concatenate([jnp.pad(gain_two_grad, ((0, 7), (0, 0))), route_grad], axis=0)
     results = to_experts(after(results, *firsts))
 
-    dqkv, table_grad = whole(
-        partial(attend_back_kernel, ranks, head_count),
-        [shape((group, 3 * heads_wide), BF), shape((16, LANES), F32)],
+    dqkv, table_grad, weight_grad = whole(
+        partial(back_and_grad_kernel, ranks, head_count),
+        [
+            shape((group, 3 * heads_wide), BF),
+            shape((16, LANES), F32),
+            shape((width, (3 + ranks) * heads_wide), BF),
+        ],
         [
             pltpu.VMEM((2, group // BLOCK, BLOCK, BLOCK), F32),
             pltpu.VMEM((2, group // BLOCK, BLOCK, BLOCK), F32),
@@ -1008,21 +1036,17 @@
             pltpu.VMEM((group, LANES), F32),
             pltpu.VMEM((group, LANES), F32),
             pltpu.VMEM((head_rows, 2 * group), F32),
+            pltpu.VMEM((width, group), BF),
         ],
         rank_arr,
-        [qkv, log_sums, offsets, lookup, *dheads],
-        20,
+        [
+            qkv, log_sums, offsets, lookup, *dheads, gain_one, dbranch, *token_pieces,
+            *attended_pieces,
+        ],
+        29,
         held=[in_own_grad, out_own_grad],
     )
-    (weight_grad,) = whole(
-        partial(project_grad_kernel, ranks),
-        [shape((width, (3 + ranks) * heads_wide), BF)],
-        [pltpu.VMEM((width, group), BF)],
-        rank_arr,
-        [gain_one, dqkv, dbranch, *token_pieces, *attended_pieces],
-        8,
-        held=[results, *thirds],
-    )
+    weight_grad = after(weight_grad, *thirds)
     core = lax.axis_index("dp") % 2
     shards = weight_grad.reshape(experts // 2, 2, width // experts, -1)
     swapped = lax.ppermute(
@@ -1043,11 +1067,11 @@
         rank_arr,
         [weights, dqkv, table_grad, *token_pieces],
         7,
-        held=[weight_grad],
+        held=[weight_grad, results],
     )
     dnormed_pieces = exchanged(after(dnormed_other, swapped))
     fourths = [
-        sent(after(grad[hidden // 2 :], *dnormed_pieces), ranks - 1 - j)
+        sent(after(grad[5 * hidden // 8 :], *dnormed_pieces), ranks - 1 - j)
         for j, grad in enumerate(out_grads)
     ]
     shards = lax.all_to_all(

time: 527 us -> 536 us (1.017)
  waiting for transfers between devices: 124 us -> 138 us
    ppermute x17, waiting for transfers between devices: 85.3 us -> 97.7 us  [sent(): lax.ppermute(values, 'mp', [(i, (i + shift) % ranks) for i in range(ranks)])]
    pallas_call x11 -> x10, Pallas kernels: 107 us -> 104 us  [whole(): pl.pallas_call(body, out_shape=outs, in_specs=[pl.BlockSpec(memory_space=...]
  transfers between devices with their start and end apart: 34 -> 34, of which waited for: 17 -> 18; matrix products, arithmetic and copies ran while one was open for 11% -> 11% of each run, Pallas kernels for 39% -> 39%
where the time goes in v3:
time: 536 us; the launch traced here: 530 us
  Pallas kernels  208 us (39%)
  waiting for transfers between devices  138 us (26%)
  starting transfers between devices  88.1 us (16%)
  local copies, waits for them, and re-layouts  35.7 us (7%)
  matrix products  32.9 us (6%)
  between operations  14.9 us (3%)
  other arithmetic  12.9 us (2%)
    pallas_call x10, Pallas kernels, whole(): pl.pallas_call(body, out_shape=outs, in_specs=[pl.BlockSpec(memory_space=...  104 us
    ppermute x17, waiting for transfers between devices, sent(): lax.ppermute(values, 'mp', [(i, (i + shift) % ranks) for i in range(ranks)])  97.7 us
    pallas_call x3, Pallas kernels, expert_call(): pl.pallas_call(partial(expert_kernel, steps, experts, chunk * slots, firs...  77.8 us
    all_to_all x7, starting transfers between devices, to_experts(): return lax.all_to_all(rows, 'dp', split_axis=0, concat_axis=0, tiled=True)  52.3 us
    dot_general x5, matrix products, rows_dot(): lax.dot_general(left, right, (((0,), (0,)), ((), ())), preferred_element_...  32.9 us
    all_to_all x7, waiting for transfers between devices, to_experts(): return lax.all_to_all(rows, 'dp', split_axis=0, concat_axis=0, tiled=True)  25.9 us
    ppermute x17, starting transfers between devices, sent(): lax.ppermute(values, 'mp', [(i, (i + shift) % ranks) for i in range(ranks)])  23.2 us
    unnamed x87, local copies, waits for them, and re-layouts  21.1 us
  transfers between devices with their start and end apart: 34, of which 18 were waited for; matrix products, arithmetic and copies ran while one was open for 11% of the time, Pallas kernels for 39%

profile of v3, /device:TPU:0, one launch (start us, length us, event | category | flops | bytes accessed | tf_op | source)
XLA Modules:
  0.0 530.3 jit_solution(8992344132744276748)
XLA Ops:
  44.1 7.4 %collective-permute-done.5.refs_3_ = bf16[512,768]{1,0:T(8,128)(2,1)S(1)} collective-permute-done((bf16[512,768]{1,0:T(8,128)(2,1)}, bf16[512,768]{1,0:T(8,128)(2,1)S(1)}, u32[]{:S(2)}, u32[]{:S(2)}) %collective-permute-start.5) | collective-permute-done | bytes 786464 | tf_op jit(solution)/shard_map/ppermute | solution.py:852
  52.4 9.3 %shard_map.203.refs_0_ = bf16[16,128,768]{2,1,0:T(8,128)(2,1)} custom-call(s32[1]{0:T(128)} %bitcast.refs_0_, f32[16,1024]{1,0:T(8,128)} %get-tuple-element.67.refs_2_.refs_1_, bf16[512,768]{1,0:T(8,128)(2,1)} %refs_3_.3, bf16[512,768]{1,0:T(8,128)(2,1)} %copy-done.36, bf16[16,16,128]{2,1,0:T(8,128)(2,1)} %copy-done.27, bf16[512,768]{1,0:T(8,128)(2,1)} %copy-done.25, ...), custom_call_target="tpu_custom_call" | custom-call | flops 9900000256 | tf_op jit(solution)/shard_map/pallas_call | solution.py:52
  72.8 16.4 %shard_map.196 = (bf16[1024,1152]{1,0:T(8,128)(2,1)}, bf16[1024,384]{1,0:T(8,128)(2,1)}, f32[8,1024]{1,0:T(8,128)}, f32[16,2048]{1,0:T(8,128)}) custom-call(s32[1]{0:T(128)} %bitcast.refs_0_, f32[1,768]{1,0:T(1,128)} %reshape.63.refs_1_.refs_7_, bf16[768,1920]{1,0:T(8,128)(2,1)} %all-gather.2.cloned.1.call-done.refs_2_.refs_1_, ...), custom_call_target="tpu_custom_call" | custom-call | flops 17600000000 | tf_op jit(solution)/shard_map/pallas_call | solution.py:52
  91.3 8.7 %collective-permute-done.3.refs_1_ = bf16[768,768]{1,0:T(8,128)(2,1)} collective-permute-done((bf16[768,768]{1,0:T(8,128)(2,1)}, bf16[768,768]{1,0:T(8,128)(2,1)}, u32[]{:S(2)}, u32[]{:S(2)}) %collective-permute-start.3) | collective-permute-done | bytes 1179680 | tf_op jit(solution)/shard_map/ppermute | solution.py:852
  104.5 15.0 %collective-permute-done.4.refs_6_.refs_1_.refs_12_ = bf16[1024,384]{1,0:T(8,128)(2,1)} collective-permute-done((bf16[1024,384]{1,0:T(8,128)(2,1)}, bf16[1024,384]{1,0:T(8,128)(2,1)}, u32[]{:S(2)}, u32[]{:S(2)}) %collective-permute-start.4) | collective-permute-done | bytes 786464 | tf_op jit(solution)/shard_map/ppermute | solution.py:852
  121.0 12.3 %shard_map.201 = (f32[512,768]{1,0:T(8,128)}, bf16[16,64,768]{2,1,0:T(8,128)(2,1)}, bf16[16,64,768]{2,1,0:T(8,128)(2,1)}) custom-call(s32[1]{0:T(128)} %bitcast.refs_0_, f32[1,768]{1,0:T(1,128)} %reshape.61.refs_1_, f32[16,1024]{1,0:T(8,128)} %get-tuple-element.67.refs_2_.refs_1_, bf16[512,768]{1,0:T(8,128)(2,1)} %refs_2_.3, bf16[512,768]{1,0:T(8,128)(2,1)} %copy-done.25, ...), custom_call_target="tpu_custom_call" | custom-call | flops 13200000000 | tf_op jit(solution)/shard_map/pallas_call | solution.py:52
  135.5 10.3 %all-to-all-start.2 = ((bf16[16,64,768]{2,1,0:T(8,128)(2,1)}), bf16[16,64,768]{2,1,0:T(8,128)(2,1)S(1)}, u32[]{:S(2)}, u32[]{:S(2)}) async-start(bf16[16,64,768]{2,1,0:T(8,128)(2,1)} %shard_map.206), calls=%async_computation.2 | async-start | bytes 3145728 | tf_op jit(solution)/shard_map/all_to_all | solution.py:861
  151.9 25.9 %all-to-all-done.2.refs_1_.rows_ref = bf16[16,64,768]{2,1,0:T(8,128)(2,1)S(1)} async-done(((bf16[16,64,768]{2,1,0:T(8,128)(2,1)}), bf16[16,64,768]{2,1,0:T(8,128)(2,1)S(1)}, u32[]{:S(2)}, u32[]{:S(2)}) %all-to-all-start.2) | async-done | bytes 1572896 | tf_op jit(solution)/shard_map/all_to_all | solution.py:861
  179.0 9.5 %all-to-all-start.3 = ((bf16[16,64,768]{2,1,0:T(8,128)(2,1)}), bf16[16,64,768]{2,1,0:T(8,128)(2,1)S(1)}, u32[]{:S(2)}, u32[]{:S(2)}) async-start(bf16[16,64,768]{2,1,0:T(8,128)(2,1)} %shard_map.208), calls=%async_computation.3 | async-start | bytes 3145728 | tf_op jit(solution)/shard_map/all_to_all | solution.py:861
  189.4 20.4 %shard_map.210 = (bf16[2048,768]{1,0:T(8,128)(2,1)}, bf16[2048,768]{1,0:T(8,128)(2,1)}, bf16[2,2048,1536]{2,1,0:T(8,128)(2,1)}, bf16[2,2048,1536]{2,1,0:T(8,128)...) custom-call(s32[1]{0:T(128)} %bitcast.6.ids_ref, bf16[16,64,768]{2,1,0:T(8,128)(2,1)} %copy-done.13, ...), custom_call_target="tpu_custom_call" | custom-call | flops 4400000000 | tf_op jit(solution)/shard_map/pallas_call | solution.py:456
  214.4 22.8 %shard_map.213 = (bf16[2,2048,1536]{2,1,0:T(8,128)(2,1)}, bf16[2,2048,1536]{2,1,0:T(8,128)(2,1)}, bf16[16,64,768]{2,1,0:T(8,128)(2,1)}, f32[16,768]{1,0:T(8,128)}, bf16[16,128,768]{2,1,0:T(8,128)(2,1)}) custom-call(s32[1]{0:T(128)} %bitcast.6.ids_ref, bf16[16,64,768]{2,1,0:T(8,128)(2,1)} %copy-done.13, ...), custom_call_target="tpu_custom_call", output_to_operand_aliasing={{0}: (12, {}), {1}: (13, {})} | custom-call | flops 4400000000 | tf_op jit(solution)/shard_map/pallas_call | solution.py:456
  237.2 6.7 %all-to-all-start.5 = ((bf16[16,64,768]{2,1,0:T(8,128)(2,1)}), bf16[16,64,768]{2,1,0:T(8,128)(2,1)}, u32[]{:S(2)}, u32[]{:S(2)}) async-start(bf16[16,64,768]{2,1,0:T(8,128)(2,1)} %get-tuple-element.103), calls=%async_computation.5 | async-start | bytes 3145728 | tf_op jit(solution)/shard_map/all_to_all | solution.py:861
  244.0 34.6 %shard_map.214 = (bf16[2048,768]{1,0:T(8,128)(2,1)}, bf16[2048,768]{1,0:T(8,128)(2,1)}, bf16[2,2048,1536]{2,1,0:T(8,128)(2,1)}, bf16[2,2048,1536]{2,1,0:T(8,128)...) custom-call(s32[1]{0:T(128)} %bitcast.6.ids_ref, ...), custom_call_target="tpu_custom_call", output_to_operand_aliasing={{0}: (9, {}), {1}: (10, {}), {2}: (11, {}), {3}: (12, {}), ... | custom-call | flops 38499999744 | tf_op jit(solution)/shard_map/pallas_call | solution.py:456
  278.6 6.9 %all-to-all-start.6 = ((bf16[16,64,768]{2,1,0:T(8,128)(2,1)}), bf16[16,64,768]{2,1,0:T(8,128)(2,1)}, u32[]{:S(2)}, u32[]{:S(2)}) async-start(bf16[16,64,768]{2,1,0:T(8,128)(2,1)} %get-tuple-element.104), calls=%async_computation.6 | async-start | bytes 3145728 | tf_op jit(solution)/shard_map/all_to_all | solution.py:861
  303.2 16.3 %collective-permute-done.8.refs_1_.refs_4_.refs_0_ = bf16[384,1536]{1,0:T(8,128)(2,1)S(1)} collective-permute-done((bf16[384,1536]{1,0:T(8,128)(2,1)S(1)}, bf16[384,1536]{1,0:T(8,128)(2,1)S(1)}, u32[]{:S(2)}, u32[]{:S(2)}) %collective-permute-start.8) | collective-permute-done | bytes 1179680 | tf_op jit(solution)/shard_map/ppermute | solution.py:852
  328.1 8.1 %shard_map.216 = (f32[512,768]{1,0:T(8,128)}, bf16[1,512,768]{2,1,0:T(8,128)(2,1)}) custom-call(s32[1]{0:T(128)} %bitcast.refs_0_, f32[1024,128]{1,0:T(8,128)} %get-tuple-element.72.refs_1_, bf16[16,64,768]{2,1,0:T(8,128)(2,1)} %all-to-all-done.5.refs_2_, bf16[16,64,768]{2,1,0:T(8,128)(2,1)} %all-to-all-done.6.refs_3_, bf16[384,1536]{1,0:T(8,128)(2,1)} %copy-done.2, ...), custom_call_target="tpu_custom_call" | custom-call | flops 8800000000 | tf_op jit(solution)/shard_map/pallas_call | solution.py:52
  337.9 9.6 %fusion.2.refs_13_.own_ref = f32[768,1536]{1,0:T(8,128)} fusion(bf16[2048,768]{1,0:T(8,128)(2,1)} %shard_map.219, bf16[2,2048,1536]{2,1,0:T(8,128)(2,1)} %get-tuple-element.99), kind=kOutput, calls=%fused_computation.2 | convolution fusion | flops 4831838208 | bytes 14155776 | tf_op jit(solution)/shard_map/dot_general | solution.py:983
  349.6 15.6 %collective-permute-done.9.refs_5_ = bf16[512,768]{1,0:T(8,128)(2,1)S(1)} collective-permute-done((bf16[512,768]{1,0:T(8,128)(2,1)S(1)}, bf16[512,768]{1,0:T(8,128)(2,1)S(1)}, u32[]{:S(2)}, u32[]{:S(2)}) %collective-permute-start.9) | collective-permute-done | bytes 786464 | tf_op jit(solution)/shard_map/ppermute | solution.py:852
  373.2 8.7 %fusion.refs_14_.own_ref = f32[1536,768]{1,0:T(8,128)} fusion(bf16[2048,768]{1,0:T(8,128)(2,1)S(1)} %copy-done.15, bf16[2,2048,1536]{2,1,0:T(8,128)(2,1)} %get-tuple-element.105), kind=kOutput, calls=%fused_computation | convolution fusion | flops 4831838208 | bytes 14155776 | tf_op jit(solution)/shard_map/dot_general | solution.py:983
  384.1 26.7 %shard_map.221 = (bf16[1024,1152]{1,0:T(8,128)(2,1)}, f32[16,128]{1,0:T(8,128)}, bf16[768,1920]{1,0:T(8,128)(2,1)}) custom-call(s32[1]{0:T(128)} %bitcast.refs_0_, bf16[1024,1152]{1,0:T(8,128)(2,1)} %get-tuple-element.100.refs_1_, f32[8,1024]{1,0:T(8,128)} %get-tuple-element.101.refs_2_, f32[16,2048]{1,0:T(8,128)} %get-tuple-element.102.refs_3_, ...), custom_call_target="tpu_custom_call" | custom-call | flops 31900000256 | tf_op jit(solution)/shard_map/pallas_call | solution.py:52
  431.5 7.3 %shard_map.224 = (f32[512,768]{1,0:T(8,128)}, bf16[1,512,768]{2,1,0:T(8,128)(2,1)}, f32[24,768]{1,0:T(8,128)}) custom-call(s32[1]{0:T(128)} %bitcast.refs_0_, bf16[768,1920]{1,0:T(8,128)(2,1)} %all-gather.2.cloned.1.call-done.refs_2_.refs_1_, bf16[1024,1152]{1,0:T(8,128)(2,1)} %get-tuple-element.112.refs_2_, f32[16,128]{1,0:T(8,128)} %get-tuple-element.113.refs_3_, ...), custom_call_target="tpu_custom_call" | custom-call | flops 7699999744 | tf_op jit(solution)/shard_map/pallas_call | solution.py:52
  441.7 16.7 %collective-permute-done.14.refs_3_.refs_5_.refs_1_ = bf16[512,768]{1,0:T(8,128)(2,1)S(1)} collective-permute-done((bf16[512,768]{1,0:T(8,128)(2,1)}, bf16[512,768]{1,0:T(8,128)(2,1)S(1)}, u32[]{:S(2)}, u32[]{:S(2)}) %collective-permute-start.14) | collective-permute-done | bytes 786464 | tf_op jit(solution)/shard_map/ppermute | solution.py:852
  459.2 8.4 %shard_map.226 = (f32[512,768]{1,0:T(8,128)}, bf16[1,512,768]{2,1,0:T(8,128)(2,1)}) custom-call(s32[1]{0:T(128)} %bitcast.refs_0_, f32[1024,128]{1,0:T(8,128)} %get-tuple-element.72.refs_1_, bf16[16,128,768]{2,1,0:T(8,128)(2,1)} %all-to-all-done.4.refs_7_.refs_2_, bf16[512,768]{1,0:T(8,128)(2,1)} %copy-done.18), custom_call_target="tpu_custom_call" | custom-call | tf_op jit(solution)/shard_map/pallas_call | solution.py:52
  498.2 7.1 %collective-permute-done.22.refs_2_.refs_1_ = bf16[576,768]{1,0:T(8,128)(2,1)S(1)} collective-permute-done((bf16[576,768]{1,0:T(8,128)(2,1)}, bf16[576,768]{1,0:T(8,128)(2,1)S(1)}, u32[]{:S(2)}, u32[]{:S(2)}) %collective-permute-start.22) | collective-permute-done | bytes 884768 | tf_op jit(solution)/shard_map/ppermute | solution.py:852
  (203 shorter events, 184.7 us)
Async XLA Ops:
  7.2 54.9 %all-gather.2.cloned.1.call-start = ((), (), s32[]{:S(2)}) async-start(), calls=%async_computation.8 | async-start | bytes 3133440 | tf_op jit(solution)/shard_map/all_gather | solution.py:888
  13.9 27.9 %collective-permute-start = (bf16[512,768]{1,0:T(8,128)(2,1)}, bf16[512,768]{1,0:T(8,128)(2,1)S(1)}, u32[]{:S(2)}, u32[]{:S(2)}) collective-permute-start(bf16[512,768]{1,0:T(8,128)(2,1)} %refs_2_.3), channel_id=1, source_target_pairs={{0,1},{1,0},{2,3},{3,2},{4,5},{5,4},{6,7},{7,6},{8,9},{9,8},{10,11... | collective-permute-start | bytes 2359304 | tf_op jit(solution)/shard_map/ppermute | solution.py:852
  16.0 35.5 %collective-permute-start.5 = (bf16[512,768]{1,0:T(8,128)(2,1)}, bf16[512,768]{1,0:T(8,128)(2,1)S(1)}, u32[]{:S(2)}, u32[]{:S(2)}) collective-permute-start(bf16[512,768]{1,0:T(8,128)(2,1)} %refs_3_.3), channel_id=1, source_target_pairs={{0,1},{1,0},{2,3},{3,2},{4,5},{5,4},{6,7},{7,6},{8,9},{9,8},{10,11... | collective-permute-start | bytes 2359304 | tf_op jit(solution)/shard_map/ppermute | solution.py:852
  23.4 20.6 %all-to-all-start = ((bf16[16,16,128]{2,1,0:T(8,128)(2,1)}), bf16[16,16,128]{2,1,0:T(8,128)(2,1)S(1)}, u32[]{:S(2)}, u32[]{:S(2)}) async-start(bf16[16,16,128]{2,1,0:T(8,128)(2,1)} %get-tuple-element.75), calls=%async_computation | async-start | bytes 131072 | tf_op jit(solution)/shard_map/all_to_all | solution.py:861
  42.7 19.4 %collective-permute-start.2 = (bf16[768,384]{1,0:T(8,128)(2,1)}, bf16[768,384]{1,0:T(8,128)(2,1)S(1)}, u32[]{:S(2)}, u32[]{:S(2)}) collective-permute-start(bf16[768,384]{1,0:T(8,128)(2,1)} %shard_map.198), channel_id=1, source_target_pairs={{0,1},{1,0},{2,3},{3,2},{4,5},{5,4},{6,7},{7,6},{8,9},{9,8},{10,11... | collective-permute-start | bytes 1769480 | tf_op jit(solution)/shard_map/ppermute | solution.py:852
  62.9 71.0 %all-to-all-start.1 = ((bf16[16,128,768]{2,1,0:T(8,128)(2,1)}), bf16[16,128,768]{2,1,0:T(8,128)(2,1)S(1)}, u32[]{:S(2)}, u32[]{:S(2)}) async-start(bf16[16,128,768]{2,1,0:T(8,128)(2,1)} %shard_map.204), calls=%async_computation.1 | async-start | bytes 6291456 | tf_op jit(solution)/shard_map/all_to_all | solution.py:861
  71.3 28.7 %collective-permute-start.3 = (bf16[768,768]{1,0:T(8,128)(2,1)}, bf16[768,768]{1,0:T(8,128)(2,1)}, u32[]{:S(2)}, u32[]{:S(2)}) collective-permute-start(bf16[768,768]{1,0:T(8,128)(2,1)} %shard_map.199), channel_id=1, source_target_pairs={{0,1},{1,0},{2,3},{3,2},{4,5},{5,4},{6,7},{7,6},{8,9},{9,8},{10,11... | collective-permute-start | bytes 3538952 | tf_op jit(solution)/shard_map/ppermute | solution.py:852
  100.0 19.5 %collective-permute-start.4 = (bf16[1024,384]{1,0:T(8,128)(2,1)}, bf16[1024,384]{1,0:T(8,128)(2,1)}, u32[]{:S(2)}, u32[]{:S(2)}) collective-permute-start(bf16[1024,384]{1,0:T(8,128)(2,1)} %shard_map.200), channel_id=1, source_target_pairs={{0,1},{1,0},{2,3},{3,2},{4,5},{5,4},{6,7},{7,6},{8,9},{9,8},{10,11... | collective-permute-start | bytes 2359304 | tf_op jit(solution)/shard_map/ppermute | solution.py:852
  119.5 14.4 %collective-permute-start.6 = (bf16[768,384]{1,0:T(8,128)(2,1)}, bf16[768,384]{1,0:T(8,128)(2,1)}, u32[]{:S(2)}, u32[]{:S(2)}) collective-permute-start(bf16[768,384]{1,0:T(8,128)(2,1)} %shard_map.205), channel_id=1, source_target_pairs={{0,1},{1,0},{2,3},{3,2},{4,5},{5,4},{6,7},{7,6},{8,9},{9,8},{10,11... | collective-permute-start | bytes 1769480 | tf_op jit(solution)/shard_map/ppermute | solution.py:852
  135.5 42.3 %all-to-all-start.2 = ((bf16[16,64,768]{2,1,0:T(8,128)(2,1)}), bf16[16,64,768]{2,1,0:T(8,128)(2,1)S(1)}, u32[]{:S(2)}, u32[]{:S(2)}) async-start(bf16[16,64,768]{2,1,0:T(8,128)(2,1)} %shard_map.206), calls=%async_computation.2 | async-start | bytes 3145728 | tf_op jit(solution)/shard_map/all_to_all | solution.py:861
  145.9 63.9 %collective-permute-start.7 = (bf16[1536,768]{1,0:T(8,128)(2,1)}, bf16[1536,768]{1,0:T(8,128)(2,1)}, u32[]{:S(2)}, u32[]{:S(2)}) collective-permute-start(bf16[1536,768]{1,0:T(8,128)(2,1)} %shard_map.209), channel_id=1, source_target_pairs={{0,1},{1,0},{2,3},{3,2},{4,5},{5,4},{6,7},{7,6},{8,9},{9,8},{10,11... | collective-permute-start | bytes 7077896 | tf_op jit(solution)/shard_map/ppermute | solution.py:852
  179.0 58.2 %all-to-all-start.3 = ((bf16[16,64,768]{2,1,0:T(8,128)(2,1)}), bf16[16,64,768]{2,1,0:T(8,128)(2,1)S(1)}, u32[]{:S(2)}, u32[]{:S(2)}) async-start(bf16[16,64,768]{2,1,0:T(8,128)(2,1)} %shard_map.208), calls=%async_computation.3 | async-start | bytes 3145728 | tf_op jit(solution)/shard_map/all_to_all | solution.py:861
  237.2 41.3 %all-to-all-start.5 = ((bf16[16,64,768]{2,1,0:T(8,128)(2,1)}), bf16[16,64,768]{2,1,0:T(8,128)(2,1)}, u32[]{:S(2)}, u32[]{:S(2)}) async-start(bf16[16,64,768]{2,1,0:T(8,128)(2,1)} %get-tuple-element.103), calls=%async_computation.5 | async-start | bytes 3145728 | tf_op jit(solution)/shard_map/all_to_all | solution.py:861
  278.6 43.5 %all-to-all-start.6 = ((bf16[16,64,768]{2,1,0:T(8,128)(2,1)}), bf16[16,64,768]{2,1,0:T(8,128)(2,1)}, u32[]{:S(2)}, u32[]{:S(2)}) async-start(bf16[16,64,768]{2,1,0:T(8,128)(2,1)} %get-tuple-element.104), calls=%async_computation.6 | async-start | bytes 3145728 | tf_op jit(solution)/shard_map/all_to_all | solution.py:861
  291.1 28.4 %collective-permute-start.8 = (bf16[384,1536]{1,0:T(8,128)(2,1)S(1)}, bf16[384,1536]{1,0:T(8,128)(2,1)S(1)}, u32[]{:S(2)}, u32[]{:S(2)}) collective-permute-start(bf16[384,1536]{1,0:T(8,128)(2,1)S(1)} %fusion.19), channel_id=1, source_target_pairs={{0,1},{1,0},{2,3},{3,2},{4,5},{5,4},{6,7},{7,6},{8,9},{9,8},{10,11... | collective-permute-start | bytes 3538952 | tf_op jit(solution)/shard_map/ppermute | solution.py:852
  320.5 29.1 %collective-permute-start.10 = (bf16[384,1536]{1,0:T(8,128)(2,1)}, bf16[384,1536]{1,0:T(8,128)(2,1)S(1)}, u32[]{:S(2)}, u32[]{:S(2)}) collective-permute-start(bf16[384,1536]{1,0:T(8,128)(2,1)} %shard_map.217), channel_id=1, source_target_pairs={{0,1},{1,0},{2,3},{3,2},{4,5},{5,4},{6,7},{7,6},{8,9},{9,8},{10,11... | collective-permute-start | bytes 3538952 | tf_op jit(solution)/shard_map/ppermute | solution.py:852
  322.0 104.1 %all-to-all-start.4 = ((bf16[16,128,768]{2,1,0:T(8,128)(2,1)}), bf16[16,128,768]{2,1,0:T(8,128)(2,1)}, u32[]{:S(2)}, u32[]{:S(2)}) async-start(bf16[16,128,768]{2,1,0:T(8,128)(2,1)} %shard_map.215), calls=%async_computation.4 | async-start | bytes 6291456 | tf_op jit(solution)/shard_map/all_to_all | solution.py:861
  337.3 27.9 %collective-permute-start.9 = (bf16[512,768]{1,0:T(8,128)(2,1)S(1)}, bf16[512,768]{1,0:T(8,128)(2,1)S(1)}, u32[]{:S(2)}, u32[]{:S(2)}) collective-permute-start(bf16[512,768]{1,0:T(8,128)(2,1)S(1)} %bitcast.77), channel_id=1, source_target_pairs={{0,1},{1,0},{2,3},{3,2},{4,5},{5,4},{6,7},{7,6},{8,9},{9,8},{10,11... | collective-permute-start | bytes 2359304 | tf_op jit(solution)/shard_map/ppermute | solution.py:852
  382.7 33.1 %collective-permute-start.12 = (bf16[960,768]{1,0:T(8,128)(2,1)}, bf16[960,768]{1,0:T(8,128)(2,1)S(1)}, u32[]{:S(2)}, u32[]{:S(2)}) collective-permute-start(bf16[960,768]{1,0:T(8,128)(2,1)} %shard_map.222), channel_id=1, source_target_pairs={{0,1},{1,0},{2,3},{3,2},{4,5},{5,4},{6,7},{7,6},{8,9},{9,8},{10,11... | collective-permute-start | bytes 4423688 | tf_op jit(solution)/shard_map/ppermute | solution.py:852
  426.1 90.1 %all-to-all-start.7 = ((bf16[8,48,1920]{2,1,0:T(8,128)(2,1)}), bf16[8,48,1920]{2,1,0:T(8,128)(2,1)}, u32[]{:S(2)}, u32[]{:S(2)}) async-start(bf16[8,48,1920]{2,1,0:T(8,128)(2,1)} %fusion.18), calls=%async_computation.7 | async-start | bytes 2949120 | tf_op jit(solution)/shard_map/all_to_all | solution.py:1077
  438.8 19.5 %collective-permute-start.14 = (bf16[512,768]{1,0:T(8,128)(2,1)}, bf16[512,768]{1,0:T(8,128)(2,1)S(1)}, u32[]{:S(2)}, u32[]{:S(2)}) collective-permute-start(bf16[512,768]{1,0:T(8,128)(2,1)} %bitcast.67), channel_id=1, source_target_pairs={{0,1},{1,0},{2,3},{3,2},{4,5},{5,4},{6,7},{7,6},{8,9},{9,8},{10,11... | collective-permute-start | bytes 2359304 | tf_op jit(solution)/shard_map/ppermute | solution.py:852
  467.6 30.5 %collective-permute-start.15 = (bf16[512,768]{1,0:T(8,128)(2,1)}, bf16[512,768]{1,0:T(8,128)(2,1)}, u32[]{:S(2)}, u32[]{:S(2)}) collective-permute-start(bf16[512,768]{1,0:T(8,128)(2,1)} %bitcast.76), channel_id=1, source_target_pairs={{0,1},{1,0},{2,3},{3,2},{4,5},{5,4},{6,7},{7,6},{8,9},{9,8},{10,11... | collective-permute-start | bytes 2359304 | tf_op jit(solution)/shard_map/ppermute | solution.py:852
  468.2 37.1 %collective-permute-start.22 = (bf16[576,768]{1,0:T(8,128)(2,1)}, bf16[576,768]{1,0:T(8,128)(2,1)S(1)}, u32[]{:S(2)}, u32[]{:S(2)}) collective-permute-start(bf16[576,768]{1,0:T(8,128)(2,1)} %shard_map.229), channel_id=1, source_target_pairs={{0,1},{1,0},{2,3},{3,2},{4,5},{5,4},{6,7},{7,6},{8,9},{9,8},{10,11... | collective-permute-start | bytes 2654216 | tf_op jit(solution)/shard_map/ppermute | solution.py:852
  480.8 13.6 %collective-permute-start.21 = (f32[48,768]{1,0:T(8,128)S(1)}, f32[48,768]{1,0:T(8,128)S(1)}, u32[]{:S(2)}, u32[]{:S(2)}) collective-permute-start(f32[48,768]{1,0:T(8,128)S(1)} %add_add_fusion.1), channel_id=1, source_target_pairs={{0,24},{2,26},{4,28},{6,30},{8,16},{10,18},{12,20},{14,22},{16,8},... | collective-permute-start | bytes 442376 | tf_op jit(solution)/shard_map/ppermute | solution.py:871
  (52 other events, 420.6 us)
Sparse Core Ops, SparseCore 0:
  14.0 46.4 all-gather.1
